TPU v7x, 128 devices: a whole 4x4x4 slice. The times are simulated.
128 devices in a mesh: seq: 32 (over x, y, core), head: 4 (over z).
Axes of the slice: x: 4, y: 4, z: 4, core: 2. Of those that a mesh axis runs over, the one named last changes fastest.
Arguments:
- queries: bfloat16 [65536, 4096], P('seq', 'head'), may hold values from -8 to 8
- keys: bfloat16 [65536, 4096], P('seq', 'head'), may hold values from -8 to 8
- values: bfloat16 [65536, 4096], P('seq', 'head'), may hold values from -10 to 10
- gain: float32 [4096], P('head'), may hold values from 0.5 to 1.5
Outputs:
- mixed: bfloat16 [65536, 4096], P('seq', 'head')
All inputs are finite; a program needn't handle non-finite values.
Results may differ from a plain program's by a relative error of at most 0.034.
Values may be sent and summed in bfloat16 or wider, within the bound.
No kernel may reach another device: no remote copies, remote signals or barrier semaphores. Data moves between devices by JAX's collectives and lax.ppermute only.
A program may use at most 192 MiB of HBM per device.

v0:
```python
import functools
import math

import jax
import jax.numpy as jnp
from jax import lax
from jax.experimental import pallas as pl
from jax.experimental.pallas import tpu as pltpu
from jax.sharding import PartitionSpec as P

HEAD_DIM = 128
BLOCK = 128
GROUP = 256
LOG2_SCALE = math.log2(math.e) / math.sqrt(HEAD_DIM)
F32 = jnp.float32
BF16 = jnp.bfloat16
NT = (((1,), (1,)), ((), ()))
MIB = 1 << 20


def iota2(shape, dim):
    return lax.broadcasted_iota(jnp.int32, shape, dim)


def averaging(levels, width):
    parts = []
    for level in levels:
        shape = (width >> level, width)
        hit = (iota2(shape, 1) >> level) == iota2(shape, 0)
        parts.append(jnp.where(hit, 2.0**-level, 0.0))
    return jnp.concatenate(parts, axis=0).astype(BF16)


def slab_order(rows, slabs):
    shape = (rows, rows)
    per = rows // slabs
    row = iota2(shape, 0)
    source = (row % per) * slabs + row // per
    return jnp.where(iota2(shape, 1) == source, 1.0, 0.0).astype(BF16)


def twice(array, per):
    count, width = array.shape[0] // per, array.shape[1]
    wide = jnp.broadcast_to(array.reshape(count, 1, per, width), (count, 2, per, width))
    return wide.reshape(2 * count * per, width)


def halve_slabs(array, per):
    count, width = array.shape[0] // (2 * per), array.shape[1]
    pairs = array.reshape(count, 2, per, width)
    return ((pairs[:, 0] + pairs[:, 1]) * 0.5).reshape(count * per, width)


def level_step(q, k, v, coarse, per):
    scores = lax.dot_general(q, k, NT, preferred_element_type=F32)
    peak = jnp.max(scores, axis=1, keepdims=True)
    if coarse is not None:
        coarse_peak, coarse_norm, coarse_value = coarse
        coarse_peak = twice(coarse_peak, per)
        peak = jnp.maximum(peak, coarse_peak)
    weights = jnp.exp2((scores - peak) * LOG2_SCALE)
    norm = jnp.sum(weights, axis=1, keepdims=True)
    value = jnp.dot(weights.astype(BF16), v, preferred_element_type=F32)
    if coarse is not None:
        scale = 2.0 * jnp.exp2((coarse_peak - peak) * LOG2_SCALE)
        norm = norm + scale * twice(coarse_norm, per)
        value = value + scale * twice(coarse_value, per)
    return peak, norm, value


def pool_kernel(k_ref, v_ref, k1, v1, k2, v2, k3, v3, kv4, kv5, kv6, kv7, kv8, mat, mat2):
    step = pl.program_id(0)

    @pl.when(step == 0)
    def _():
        mat[...] = jnp.concatenate([averaging((1, 2, 3, 4), GROUP), jnp.zeros((16, GROUP), BF16)], axis=0)
        mat2[...] = jnp.concatenate([averaging((1, 2, 3, 4), BLOCK), jnp.zeros((8, BLOCK), BF16)], axis=0)

    for index, (ref, o1, o2, o3) in enumerate(((k_ref, k1, k2, k3), (v_ref, v1, v2, v3))):
        pooled = jnp.dot(mat[...], ref[...], preferred_element_type=F32).astype(BF16)
        o1[...] = pooled[:128]
        o2[...] = pooled[128:192]
        o3[...] = pooled[192:224]
        kv4[index, pl.ds(pl.multiple_of(step * 16, 16), 16), :] = pooled[224:240]

    @pl.when(step == pl.num_programs(0) - 1)
    def _():
        for index in range(2):
            pooled = jnp.dot(mat2[...], kv4[index], preferred_element_type=F32).astype(BF16)
            kv5[index] = pooled[:64]
            kv6[index] = pooled[64:96]
            kv7[index] = pooled[96:112]
            kv8[index] = pooled[112:128]


def pool(keys, values):
    rows, width = keys.shape
    groups = rows // GROUP
    shapes = []
    specs = []
    for level in (1, 2, 3):
        for _ in range(2):
            shapes.append(jax.ShapeDtypeStruct((rows >> level, width), BF16))
            specs.append(pl.BlockSpec((GROUP >> level, width), lambda g: (g, 0)))
    for count in (128, 64, 32, 16, 16):
        shapes.append(jax.ShapeDtypeStruct((2, count, width), BF16))
        specs.append(pl.BlockSpec((2, count, width), lambda g: (0, 0, 0)))
    block = pl.BlockSpec((GROUP, width), lambda g: (g, 0))
    return pl.pallas_call(
        pool_kernel,
        grid=(groups,),
        in_specs=[block, block],
        out_specs=specs,
        out_shape=shapes,
        scratch_shapes=[pltpu.VMEM((GROUP, GROUP), BF16), pltpu.VMEM((BLOCK, BLOCK), BF16)],
        compiler_params=pltpu.CompilerParams(vmem_limit_bytes=32 * MIB),
        cost_estimate=pl.CostEstimate(flops=2 * 2 * rows * GROUP * width, bytes_accessed=15 * MIB, transcendentals=0),
        name="pool",
    )(keys, values)


def near_kernel(q_ref, k0, v0, k1, v1, k2, v2, k3, v3, *rest):
    att_ref, log_ref, q4_ref, perm = rest[-4:]

    @pl.when(pl.program_id(0) == 0)
    def _():
        perm[...] = slab_order(GROUP, 16)

    heads = q_ref.shape[1] // HEAD_DIM
    lane = iota2((GROUP, HEAD_DIM), 1)
    logs = jnp.zeros((GROUP, HEAD_DIM), F32)
    for head in range(heads):
        cols = slice(head * HEAD_DIM, (head + 1) * HEAD_DIM)
        level = jnp.dot(perm[...], q_ref[:, cols], preferred_element_type=F32)
        queries = [level.astype(BF16)]
        for _ in range(4):
            level = halve_slabs(level, 16).astype(BF16)
            queries.append(level)
            level = level.astype(F32)
        q4_ref[:, cols] = queries[4]
        state = None
        for q, k, v in ((queries[3], k3, v3), (queries[2], k2, v2), (queries[1], k1, v1), (queries[0], k0, v0)):
            state = level_step(q, k[:, cols], v[:, cols], state, 16)
        peak, norm, value = state
        att_ref[:, cols] = (value * (1.0 / norm)).astype(BF16)
        logs = jnp.where(lane == head, peak * LOG2_SCALE + jnp.log2(norm), logs)
    log_ref[...] = logs


def near(queries, keys, values, pooled, start, count, previous):
    rows, width = queries.shape
    own = pl.BlockSpec((GROUP, width), lambda g: (start + g, 0))
    specs = [own, own, own]
    for level in (1, 2, 3):
        spec = pl.BlockSpec((BLOCK, width), lambda g, s=level - 1: (((start + g) >> s) ^ 1, 0))
        specs += [spec, spec]
    aliases = {}
    if previous is not None:
        aliases = {9: 0, 10: 1, 11: 2}
        specs += [pl.BlockSpec(memory_space=pl.ANY)] * 3
    return pl.pallas_call(
        near_kernel,
        grid=(count,),
        in_specs=specs,
        out_specs=[
            own,
            pl.BlockSpec((GROUP, HEAD_DIM), lambda g: (start + g, 0)),
            pl.BlockSpec((16, width), lambda g: (start + g, 0)),
        ],
        out_shape=[
            jax.ShapeDtypeStruct((rows, width), BF16),
            jax.ShapeDtypeStruct((rows, HEAD_DIM), F32),
            jax.ShapeDtypeStruct((rows >> 4, width), BF16),
        ],
        scratch_shapes=[pltpu.VMEM((GROUP, GROUP), BF16)],
        input_output_aliases=aliases,
        compiler_params=pltpu.CompilerParams(vmem_limit_bytes=40 * MIB),
        cost_estimate=pl.CostEstimate(
            flops=count * 8 * 2 * 2 * GROUP * GROUP * 256, bytes_accessed=count * 3 * MIB, transcendentals=count * 8 * 98304
        ),
        name="near",
    )(queries, keys, values, *pooled, *(previous or ()))


def far_kernel(
    q4_ref, s4, x_own, y2_own, y4_own, y6_own, x_far, y2_far, y4_far, y6_far, near_ref, log_ref,
    att_ref, sq_ref, coarse, coarse_log,
):
    step = pl.program_id(0)
    heads = near_ref.shape[1] // HEAD_DIM

    @pl.when(step == 0)
    def _():
        lane = iota2((BLOCK, HEAD_DIM), 1)
        logs = jnp.zeros((BLOCK, HEAD_DIM), F32)
        perm = slab_order(BLOCK, 16)
        for head in range(heads):
            cols = slice(head * HEAD_DIM, (head + 1) * HEAD_DIM)
            level = jnp.dot(perm, q4_ref[:, cols], preferred_element_type=F32)
            queries = [level.astype(BF16)]
            for _ in range(4):
                level = halve_slabs(level, 8).astype(BF16)
                queries.append(level)
                level = level.astype(F32)

            def rows(parts, part):
                return jnp.concatenate([ref[part, lo:hi, cols] for ref, lo, hi in parts], axis=0)

            sides = ((x_own, y2_own, y4_own, y6_own), (x_far, y2_far, y4_far, y6_far))
            level8 = [(r, lo, hi) for x, y2, y4, y6 in sides
                      for r, lo, hi in ((x, 16, 32), (y2, 80, 96), (y4, 48, 64), (y6, 48, 64))]
            level7 = [(r, lo, hi) for x, y2, y4, y6 in sides
                      for r, lo, hi in ((x, 0, 16), (y2, 64, 80), (y4, 32, 48), (y6, 32, 48))]
            level6 = [(r, 0, 32) for x, y2, y4, y6 in sides for r in (y4, y6)]
            level5 = [(y2, 0, 64) for x, y2, y4, y6 in sides]
            state = None
            for q, parts in zip(reversed(queries), (level8, level7, level6, level5, [(s4, 0, 128)])):
                state = level_step(q, rows(parts, 0), rows(parts, 1), state, 8)
            peak, norm, value = state
            value = value * (1.0 / norm)
            for slab in range(16):
                coarse[head, pl.ds(slab, 8, stride=16), :] = value[slab * 8 : slab * 8 + 8]
            logs = jnp.where(lane == head, peak * LOG2_SCALE + jnp.log2(norm) + 4.0, logs)
        for slab in range(16):
            coarse_log[pl.ds(slab, 8, stride=16), :] = logs[slab * 8 : slab * 8 + 8]

    here = pl.ds(pl.multiple_of(step * 16, 16), 16)
    gap = log_ref[...].reshape(16, 16, HEAD_DIM) - coarse_log[here, :][None]
    share = 1.0 / (1.0 + jnp.exp2(gap)).reshape(GROUP, HEAD_DIM)
    squares = jnp.zeros((GROUP, HEAD_DIM), F32)
    for head in range(heads):
        cols = slice(head * HEAD_DIM, (head + 1) * HEAD_DIM)
        part = near_ref[:, cols].astype(F32)
        delta = (coarse[head, here, :][None] - part.reshape(16, 16, HEAD_DIM)).reshape(GROUP, HEAD_DIM)
        attended = part + share[:, head : head + 1] * delta
        squares = squares + attended * attended
        att_ref[:, cols] = attended.astype(BF16)
    sums = lax.dot_general(
        jnp.ones((8, HEAD_DIM), F32), squares, NT, precision=lax.Precision.HIGHEST, preferred_element_type=F32
    )
    sq_ref[pl.ds(step, 1), :] = sums[:1]


def far(q4, s4, own, other, near_att, near_log):
    rows, width = near_att.shape
    groups = rows // GROUP
    whole = [pl.BlockSpec(a.shape, lambda g, n=a.ndim: (0,) * n) for a in (q4, s4, *own, *other)]
    block = pl.BlockSpec((GROUP, width), lambda g: (g, 0))
    return pl.pallas_call(
        far_kernel,
        grid=(groups,),
        in_specs=whole + [block, pl.BlockSpec((GROUP, HEAD_DIM), lambda g: (g, 0))],
        out_specs=[block, pl.BlockSpec((groups, GROUP), lambda g: (0, 0))],
        out_shape=[jax.ShapeDtypeStruct((rows, width), BF16), jax.ShapeDtypeStruct((groups, GROUP), F32)],
        scratch_shapes=[pltpu.VMEM((width // HEAD_DIM, BLOCK, HEAD_DIM), F32), pltpu.VMEM((BLOCK, HEAD_DIM), F32)],
        compiler_params=pltpu.CompilerParams(vmem_limit_bytes=40 * MIB),
        name="far",
    )(q4, s4, *own, *other, near_att, near_log)


def norm_kernel(features, att_ref, s0, s1, s2, s3, gain_ref, out_ref, perm):
    step = pl.program_id(0)

    @pl.when(step == 0)
    def _():
        shape = (GROUP, GROUP)
        source = (iota2(shape, 0) % 16) * 16 + iota2(shape, 0) // 16
        perm[...] = jnp.where(iota2(shape, 1) == source, 1.0, 0.0)

    here = pl.ds(step, 1)
    total = (s0[here, :] + s1[here, :]) + (s2[here, :] + s3[here, :])
    scale = lax.rsqrt(total / features + 1e-06)
    matrix = (perm[...] * scale).astype(BF16)
    mixed = jnp.dot(matrix, att_ref[...], preferred_element_type=F32)
    out_ref[...] = (mixed * gain_ref[...]).astype(BF16)


def normed(att, sums, gain, features):
    rows, width = att.shape
    groups = rows // GROUP
    block = pl.BlockSpec((GROUP, width), lambda g: (g, 0))
    whole = pl.BlockSpec((groups, GROUP), lambda g: (0, 0))
    return pl.pallas_call(
        functools.partial(norm_kernel, features),
        grid=(groups,),
        in_specs=[block, whole, whole, whole, whole, pl.BlockSpec((1, width), lambda g: (0, 0))],
        out_specs=block,
        out_shape=jax.ShapeDtypeStruct((rows, width), BF16),
        scratch_shapes=[pltpu.VMEM((GROUP, GROUP), F32)],
        compiler_params=pltpu.CompilerParams(vmem_limit_bytes=32 * MIB),
        name="norm",
    )(att, *sums, gain.reshape(1, width))


def swapped(array, axis, bits):
    return lax.ppermute(array, axis, [(i, i ^ bits) for i in range(lax.axis_size(axis))])


def local(queries, keys, values, gain):
    *pooled, kv4, kv5, kv6, kv7, kv8 = pool(keys, values)
    rows8 = kv8[:, :8]
    x7 = swapped(kv7, "seq", 8)
    x8a = swapped(rows8, "seq", 16)
    x8b = swapped(rows8, "seq", 24)
    s4 = swapped(kv4, "seq", 1)
    first = near(queries, keys, values, pooled, 0, 2, None)
    x_own = jnp.concatenate([x7, x8a, x8b], axis=1)
    to2 = jnp.concatenate([kv5, x_own], axis=1)
    to46 = jnp.concatenate([kv6, x_own], axis=1)
    own = [x_own, swapped(to2, "seq", 2), swapped(to46, "seq", 4), swapped(to46, "seq", 6)]
    second = near(queries, keys, values, pooled, 2, 4, first)
    other = [swapped(a, "seq", 1) for a in own]
    near_att, near_log, q4 = near(queries, keys, values, pooled, 6, 2, second)
    att, squares = far(q4, s4, own, other, near_att, near_log)
    sums = [squares] + [
        lax.ppermute(squares, "head", [(i, (i + s) % 4) for i in range(4)]) for s in (1, 2, 3)
    ]
    return normed(att, sums, gain, lax.axis_size("head") * queries.shape[1])


def solution(mesh):
    return jax.shard_map(
        local,
        mesh=mesh,
        in_specs=(P("seq", "head"), P("seq", "head"), P("seq", "head"), P("head")),
        out_specs=P("seq", "head"),
        check_vma=False,
    )
```

profile of v0, /device:TPU:2, one launch (start us, length us, event | category | flops | bytes accessed | tf_op | source)
XLA Modules:
  0.0 126.4 jit_solution(1130226063813990731)
XLA Ops:
  0.0 0.0 copy-start
  0.0 2.2 %copy-done = bf16[2048,1024]{1,0:T(8,128)(2,1)S(1)} copy-done((bf16[2048,1024]{1,0:T(8,128)(2,1)S(1)}, bf16[2048,1024]{1,0:T(8,128)(2,1)}, u32[]{:S(2)}) %copy-start) | copy-done | bytes 4194328
  2.2 0.0 copy-start.1
  2.2 2.2 %copy-done.1 = bf16[2048,1024]{1,0:T(8,128)(2,1)S(1)} copy-done((bf16[2048,1024]{1,0:T(8,128)(2,1)S(1)}, bf16[2048,1024]{1,0:T(8,128)(2,1)}, u32[]{:S(2)}) %copy-start.1) | copy-done | bytes 4194328
  4.4 3.9 %pool.1 = (bf16[1024,1024]{1,0:T(8,128)(2,1)S(1)}, bf16[1024,1024]{1,0:T(8,128)(2,1)S(1)}, bf16[512,1024]{1,0:T(8,128)(2,1)S(1)}, bf16[512,1024]{1,0:T(8,128)(2,...) custom-call(bf16[2048,1024]{1,0:T(8,128)(2,1)S(1)} %copy-done, ...), custom_call_target="tpu_custom_call" | custom-call | flops 2147483648 | bytes 15728640 | tf_op jit(solution)/shard_map/pool/pallas_call | solution.py:109
  8.3 2.2 %collective-permute-start.2 = (bf16[2,8,1024]{2,1,0:T(8,128)(2,1)S(1)}, bf16[2,8,1024]{2,1,0:T(8,128)(2,1)S(1)}, u32[]{:S(2)}, u32[]{:S(2)}) collective-permute-start(bf16[2,8,1024]{2,1,0:T(8,128)(2,1)S(1)} %slice.3), channel_id=1, source_target_pairs={{0,64},{4,68},{8,72},{12,76},{16,80},{20,84},{24,88},{28,92},{32,9... | collective-permute-start | bytes 98312 | tf_op jit(solution)/shard_map/ppermute | solution.py:296
  10.6 0.0 collective-permute-start.3
  10.6 2.6 %collective-permute-start.1 = (bf16[2,16,1024]{2,1,0:T(8,128)(2,1)S(1)}, bf16[2,16,1024]{2,1,0:T(8,128)(2,1)S(1)}, u32[]{:S(2)}, u32[]{:S(2)}) collective-permute-start(bf16[2,16,1024]{2,1,0:T(8,128)(2,1)S(1)} %get-tuple-element.41), channel_id=1, source_target_pairs={{0,32},{4,36},{8,40},{12,44},{16,48},{20,52},{24,56},{28,60},{32,0... | collective-permute-start | bytes 196616 | tf_op jit(solution)/shard_map/ppermute | solution.py:296
  13.1 0.7 collective-permute-done.2
  13.8 0.6 collective-permute-done.3
  14.5 0.9 collective-permute-done.1
  15.4 1.7 %collective-permute-start.4 = (bf16[2,96,1024]{2,1,0:T(8,128)(2,1)S(1)}, bf16[2,96,1024]{2,1,0:T(8,128)(2,1)S(1)}, u32[]{:S(2)}, u32[]{:S(2)}) collective-permute-start(bf16[2,96,1024]{2,1,0:T(8,128)(2,1)S(1)} %pad_maximum_fusion), channel_id=1, source_target_pairs={{0,8},{4,12},{8,0},{12,4},{16,24},{20,28},{24,16},{28,20},{32,40},... | collective-permute-start | bytes 1179656 | tf_op jit(solution)/shard_map/ppermute | solution.py:296
  17.1 3.0 %collective-permute-start.5 = (bf16[2,64,1024]{2,1,0:T(8,128)(2,1)S(1)}, bf16[2,64,1024]{2,1,0:T(8,128)(2,1)S(1)}, u32[]{:S(2)}, u32[]{:S(2)}) collective-permute-start(bf16[2,64,1024]{2,1,0:T(8,128)(2,1)S(1)} %get-tuple-element.51), channel_id=1, source_target_pairs={{0,16},{4,20},{8,24},{12,28},{16,0},{20,4},{24,8},{28,12},{32,48},... | collective-permute-start | bytes 786440 | tf_op jit(solution)/shard_map/ppermute | solution.py:296
  20.1 0.2 collective-permute-start.6
  20.3 0.0 collective-permute-start
  20.3 7.2 %collective-permute-done.4.y2_own = bf16[2,96,1024]{2,1,0:T(8,128)(2,1)S(1)} collective-permute-done((bf16[2,96,1024]{2,1,0:T(8,128)(2,1)S(1)}, bf16[2,96,1024]{2,1,0:T(8,128)(2,1)S(1)}, u32[]{:S(2)}, u32[]{:S(2)}) %collective-permute-start.4) | collective-permute-done | bytes 393248 | tf_op jit(solution)/shard_map/ppermute | solution.py:296
  27.5 0.0 collective-permute-start.8
  27.5 17.4 %near.3 = (bf16[2048,1024]{1,0:T(8,128)(2,1)S(1)}, f32[2048,128]{1,0:T(8,128)S(1)}, bf16[128,1024]{1,0:T(8,128)(2,1)S(1)}) custom-call(bf16[2048,1024]{1,0:T(8,128)(2,1)} %q_ref.5, bf16[2048,1024]{1,0:T(8,128)(2,1)} %k0.5, bf16[2048,1024]{1,0:T(8,128)(2,1)} %v0.5, bf16[1024,1024]{1,0:T(8,128)(2,1)S(1)} %get-tuple-element.27.k1, ...), custom_call_target="tpu_custom_call" | custom-call | flops 1073741824 | bytes 6291456 | tf_op jit(solution)/shard_map/near/pallas_call | solution.py:161
  44.9 0.6 collective-permute-start.7
  45.5 0.0 collective-permute-done.5.y4_own
  45.5 0.1 collective-permute-start.9
  45.6 0.0 collective-permute-done.6.y6_own
  45.6 0.4 collective-permute-start.10
  46.0 33.3 %near.4 = (bf16[2048,1024]{1,0:T(8,128)(2,1)S(1)}, f32[2048,128]{1,0:T(8,128)S(1)}, bf16[128,1024]{1,0:T(8,128)(2,1)S(1)}) custom-call(bf16[2048,1024]{1,0:T(8,128)(2,1)} %q_ref.5, bf16[2048,1024]{1,0:T(8,128)(2,1)} %k0.5, bf16[2048,1024]{1,0:T(8,128)(2,1)} %v0.5, ...), custom_call_target="tpu_custom_call", output_to_operand_aliasing={{0}: (9, {}), {1}: (10, {}), {2}: (11, {})} | custom-call | flops 2147483648 | bytes 12582912 | tf_op jit(solution)/shard_map/near/pallas_call | solution.py:161
  79.3 17.4 %near.5 = (bf16[2048,1024]{1,0:T(8,128)(2,1)S(1)}, f32[2048,128]{1,0:T(8,128)S(1)}, bf16[128,1024]{1,0:T(8,128)(2,1)S(1)}) custom-call(bf16[2048,1024]{1,0:T(8,128)(2,1)} %q_ref.5, bf16[2048,1024]{1,0:T(8,128)(2,1)} %k0.5, bf16[2048,1024]{1,0:T(8,128)(2,1)} %v0.5, ...), custom_call_target="tpu_custom_call", output_to_operand_aliasing={{0}: (9, {}), {1}: (10, {}), {2}: (11, {})} | custom-call | flops 1073741824 | bytes 6291456 | tf_op jit(solution)/shard_map/near/pallas_call | solution.py:161
  96.7 0.0 copy-start.2
  96.7 0.0 collective-permute-done.7.x_far
  96.7 0.0 collective-permute-done.s4
  96.8 0.0 collective-permute-done.9.y4_far
  96.8 0.0 collective-permute-done.10.y6_far
  96.8 0.0 collective-permute-done.8.y2_far
  96.8 15.7 %far.1 = (bf16[2048,1024]{1,0:T(8,128)(2,1)S(1)}, f32[8,256]{1,0:T(8,128)S(1)}) custom-call(bf16[128,1024]{1,0:T(8,128)(2,1)S(1)} %get-tuple-element.39.q4_ref, bf16[2,128,1024]{2,1,0:T(8,128)(2,1)S(1)} %collective-permute-done.s4, bf16[2,32,1024]{2,1,0:T(8,128)(2,1)S(1)} %get-tuple-element.52.x_own, bf16[2,96,1024]{2,1,0:T(8,128)(2,1)S(1)} %collective-permute-done.4.y2_own, ...), custom_call_target="tpu_custom_call" | custom-call | tf_op jit(solution)/shard_map/far/pallas_call | solution.py:249
  112.5 2.0 %collective-permute-start.11 = (f32[8,256]{1,0:T(8,128)S(1)}, f32[8,256]{1,0:T(8,128)S(1)}, u32[]{:S(2)}, u32[]{:S(2)}) collective-permute-start(f32[8,256]{1,0:T(8,128)S(1)} %get-tuple-element.48.s0), channel_id=1, source_target_pairs={{0,1},{1,2},{2,3},{3,0},{4,5},{5,6},{6,7},{7,4},{8,9},{9,10},{10,1... | collective-permute-start | bytes 24584 | tf_op jit(solution)/shard_map/ppermute | solution.py:316
  114.4 3.6 %collective-permute-start.12 = (f32[8,256]{1,0:T(8,128)S(1)}, f32[8,256]{1,0:T(8,128)S(1)}, u32[]{:S(2)}, u32[]{:S(2)}) collective-permute-start(f32[8,256]{1,0:T(8,128)S(1)} %get-tuple-element.48.s0), channel_id=1, source_target_pairs={{0,2},{1,3},{2,0},{3,1},{4,6},{5,7},{6,4},{7,5},{8,10},{9,11},{10,... | collective-permute-start | bytes 24584 | tf_op jit(solution)/shard_map/ppermute | solution.py:316
  118.0 1.0 collective-permute-start.13
  119.0 0.0 collective-permute-done.11.s1
  119.0 0.7 collective-permute-done.12.s2
  119.7 1.9 %collective-permute-done.13.s3 = f32[8,256]{1,0:T(8,128)S(1)} collective-permute-done((f32[8,256]{1,0:T(8,128)S(1)}, f32[8,256]{1,0:T(8,128)S(1)}, u32[]{:S(2)}, u32[]{:S(2)}) %collective-permute-start.13) | collective-permute-done | bytes 8224 | tf_op jit(solution)/shard_map/ppermute | solution.py:316
  121.7 0.0 copy-done.2
  121.7 4.8 %norm.1 = bf16[2048,1024]{1,0:T(8,128)(2,1)} custom-call(bf16[2048,1024]{1,0:T(8,128)(2,1)S(1)} %get-tuple-element.47.att_ref, f32[8,256]{1,0:T(8,128)S(1)} %get-tuple-element.48.s0, f32[8,256]{1,0:T(8,128)S(1)} %collective-permute-done.11.s1, f32[8,256]{1,0:T(8,128)S(1)} %collective-permute-done.12.s2, f32[8,256]{1,0:T(8,128)S(1)} %collective-permute-done.13.s3, ...), custom_call_target="tpu_custom_call" | custom-call | tf_op jit(solution)/shard_map/norm/pallas_call | solution.py:283
  (6 shorter events, 0.1 us)
Async XLA Ops:
  0.0 2.2 %copy-start = (bf16[2048,1024]{1,0:T(8,128)(2,1)S(1)}, bf16[2048,1024]{1,0:T(8,128)(2,1)}, u32[]{:S(2)}) copy-start(bf16[2048,1024]{1,0:T(8,128)(2,1)} %k0.5) | copy-start | bytes 12582916
  2.2 2.2 %copy-start.1 = (bf16[2048,1024]{1,0:T(8,128)(2,1)S(1)}, bf16[2048,1024]{1,0:T(8,128)(2,1)}, u32[]{:S(2)}) copy-start(bf16[2048,1024]{1,0:T(8,128)(2,1)} %v0.5) | copy-start | bytes 12582916
  8.3 5.5 %collective-permute-start.2 = (bf16[2,8,1024]{2,1,0:T(8,128)(2,1)S(1)}, bf16[2,8,1024]{2,1,0:T(8,128)(2,1)S(1)}, u32[]{:S(2)}, u32[]{:S(2)}) collective-permute-start(bf16[2,8,1024]{2,1,0:T(8,128)(2,1)S(1)} %slice.3), channel_id=1, source_target_pairs={{0,64},{4,68},{8,72},{12,76},{16,80},{20,84},{24,88},{28,92},{32,9... | collective-permute-start | bytes 98312 | tf_op jit(solution)/shard_map/ppermute | solution.py:296
  10.6 3.9 %collective-permute-start.3 = (bf16[2,8,1024]{2,1,0:T(8,128)(2,1)S(1)}, bf16[2,8,1024]{2,1,0:T(8,128)(2,1)S(1)}, u32[]{:S(2)}, u32[]{:S(2)}) collective-permute-start(bf16[2,8,1024]{2,1,0:T(8,128)(2,1)S(1)} %slice.3), channel_id=1, source_target_pairs={{0,96},{4,100},{8,104},{12,108},{16,112},{20,116},{24,120},{28,124... | collective-permute-start | bytes 98312 | tf_op jit(solution)/shard_map/ppermute | solution.py:296
  10.6 4.8 %collective-permute-start.1 = (bf16[2,16,1024]{2,1,0:T(8,128)(2,1)S(1)}, bf16[2,16,1024]{2,1,0:T(8,128)(2,1)S(1)}, u32[]{:S(2)}, u32[]{:S(2)}) collective-permute-start(bf16[2,16,1024]{2,1,0:T(8,128)(2,1)S(1)} %get-tuple-element.41), channel_id=1, source_target_pairs={{0,32},{4,36},{8,40},{12,44},{16,48},{20,52},{24,56},{28,60},{32,0... | collective-permute-start | bytes 196616 | tf_op jit(solution)/shard_map/ppermute | solution.py:296
  15.4 12.1 %collective-permute-start.4 = (bf16[2,96,1024]{2,1,0:T(8,128)(2,1)S(1)}, bf16[2,96,1024]{2,1,0:T(8,128)(2,1)S(1)}, u32[]{:S(2)}, u32[]{:S(2)}) collective-permute-start(bf16[2,96,1024]{2,1,0:T(8,128)(2,1)S(1)} %pad_maximum_fusion), channel_id=1, source_target_pairs={{0,8},{4,12},{8,0},{12,4},{16,24},{20,28},{24,16},{28,20},{32,40},... | collective-permute-start | bytes 1179656 | tf_op jit(solution)/shard_map/ppermute | solution.py:296
  17.1 28.4 %collective-permute-start.5 = (bf16[2,64,1024]{2,1,0:T(8,128)(2,1)S(1)}, bf16[2,64,1024]{2,1,0:T(8,128)(2,1)S(1)}, u32[]{:S(2)}, u32[]{:S(2)}) collective-permute-start(bf16[2,64,1024]{2,1,0:T(8,128)(2,1)S(1)} %get-tuple-element.51), channel_id=1, source_target_pairs={{0,16},{4,20},{8,24},{12,28},{16,0},{20,4},{24,8},{28,12},{32,48},... | collective-permute-start | bytes 786440 | tf_op jit(solution)/shard_map/ppermute | solution.py:296
  20.1 25.5 %collective-permute-start.6 = (bf16[2,64,1024]{2,1,0:T(8,128)(2,1)S(1)}, bf16[2,64,1024]{2,1,0:T(8,128)(2,1)S(1)}, u32[]{:S(2)}, u32[]{:S(2)}) collective-permute-start(bf16[2,64,1024]{2,1,0:T(8,128)(2,1)S(1)} %get-tuple-element.51), channel_id=1, source_target_pairs={{0,24},{4,28},{8,16},{12,20},{16,8},{20,12},{24,0},{28,4},{32,56},... | collective-permute-start | bytes 786440 | tf_op jit(solution)/shard_map/ppermute | solution.py:296
  20.3 76.4 %collective-permute-start = (bf16[2,128,1024]{2,1,0:T(8,128)(2,1)S(1)}, bf16[2,128,1024]{2,1,0:T(8,128)(2,1)S(1)}, u32[]{:S(2)}, u32[]{:S(2)}) collective-permute-start(bf16[2,128,1024]{2,1,0:T(8,128)(2,1)S(1)} %get-tuple-element.40), channel_id=1, source_target_pairs={{0,4},{4,0},{8,12},{12,8},{16,20},{20,16},{24,28},{28,24},{32,36},... | collective-permute-start | bytes 1572872 | tf_op jit(solution)/shard_map/ppermute | solution.py:296
  27.5 69.2 %collective-permute-start.8 = (bf16[2,96,1024]{2,1,0:T(8,128)(2,1)S(1)}, bf16[2,96,1024]{2,1,0:T(8,128)(2,1)S(1)}, u32[]{:S(2)}, u32[]{:S(2)}) collective-permute-start(bf16[2,96,1024]{2,1,0:T(8,128)(2,1)S(1)} %collective-permute-done.4.y2_own), channel_id=1, source_target_pairs={{0,4},{4,0},{8,12},{12,8},{16,20},{20,16},{24,28},{28,24},{32,36},... | collective-permute-start | bytes 1179656 | tf_op jit(solution)/shard_map/ppermute | solution.py:296
  44.9 51.8 %collective-permute-start.7 = (bf16[2,32,1024]{2,1,0:T(8,128)(2,1)S(1)}, bf16[2,32,1024]{2,1,0:T(8,128)(2,1)S(1)}, u32[]{:S(2)}, u32[]{:S(2)}) collective-permute-start(bf16[2,32,1024]{2,1,0:T(8,128)(2,1)S(1)} %get-tuple-element.52.x_own), channel_id=1, source_target_pairs={{0,4},{4,0},{8,12},{12,8},{16,20},{20,16},{24,28},{28,24},{32,36},... | collective-permute-start | bytes 393224 | tf_op jit(solution)/shard_map/ppermute | solution.py:296
  45.5 51.3 %collective-permute-start.9 = (bf16[2,64,1024]{2,1,0:T(8,128)(2,1)S(1)}, bf16[2,64,1024]{2,1,0:T(8,128)(2,1)S(1)}, u32[]{:S(2)}, u32[]{:S(2)}) collective-permute-start(bf16[2,64,1024]{2,1,0:T(8,128)(2,1)S(1)} %collective-permute-done.5.y4_own), channel_id=1, source_target_pairs={{0,4},{4,0},{8,12},{12,8},{16,20},{20,16},{24,28},{28,24},{32,36},... | collective-permute-start | bytes 786440 | tf_op jit(solution)/shard_map/ppermute | solution.py:296
  45.6 51.2 %collective-permute-start.10 = (bf16[2,64,1024]{2,1,0:T(8,128)(2,1)S(1)}, bf16[2,64,1024]{2,1,0:T(8,128)(2,1)S(1)}, u32[]{:S(2)}, u32[]{:S(2)}) collective-permute-start(bf16[2,64,1024]{2,1,0:T(8,128)(2,1)S(1)} %collective-permute-done.6.y6_own), channel_id=1, source_target_pairs={{0,4},{4,0},{8,12},{12,8},{16,20},{20,16},{24,28},{28,24},{32,36},... | collective-permute-start | bytes 786440 | tf_op jit(solution)/shard_map/ppermute | solution.py:296
  96.7 25.0 %copy-start.2 = (f32[1024]{0:T(1024)S(1)}, f32[1024]{0:T(1024)}, u32[]{:S(2)}) copy-start(f32[1024]{0:T(1024)} %param.7) | copy-start | bytes 12292
  112.5 6.5 %collective-permute-start.11 = (f32[8,256]{1,0:T(8,128)S(1)}, f32[8,256]{1,0:T(8,128)S(1)}, u32[]{:S(2)}, u32[]{:S(2)}) collective-permute-start(f32[8,256]{1,0:T(8,128)S(1)} %get-tuple-element.48.s0), channel_id=1, source_target_pairs={{0,1},{1,2},{2,3},{3,0},{4,5},{5,6},{6,7},{7,4},{8,9},{9,10},{10,1... | collective-permute-start | bytes 24584 | tf_op jit(solution)/shard_map/ppermute | solution.py:316
  114.4 5.3 %collective-permute-start.12 = (f32[8,256]{1,0:T(8,128)S(1)}, f32[8,256]{1,0:T(8,128)S(1)}, u32[]{:S(2)}, u32[]{:S(2)}) collective-permute-start(f32[8,256]{1,0:T(8,128)S(1)} %get-tuple-element.48.s0), channel_id=1, source_target_pairs={{0,2},{1,3},{2,0},{3,1},{4,6},{5,7},{6,4},{7,5},{8,10},{9,11},{10,... | collective-permute-start | bytes 24584 | tf_op jit(solution)/shard_map/ppermute | solution.py:316
  118.0 3.7 %collective-permute-start.13 = (f32[8,256]{1,0:T(8,128)S(1)}, f32[8,256]{1,0:T(8,128)S(1)}, u32[]{:S(2)}, u32[]{:S(2)}) collective-permute-start(f32[8,256]{1,0:T(8,128)S(1)} %get-tuple-element.48.s0), channel_id=1, source_target_pairs={{0,3},{1,0},{2,1},{3,2},{4,7},{5,4},{6,5},{7,6},{8,11},{9,8},{10,9... | collective-permute-start | bytes 24584 | tf_op jit(solution)/shard_map/ppermute | solution.py:316
where the time goes:
time: 128 us; the launch traced here: 126 us
  Pallas kernels  92.5 us (72%)
  starting transfers between devices  17.3 us (14%)
  waiting for transfers between devices  12.1 us (9%)
  local copies, waits for them, and re-layouts  4.42 us (3%)
    pallas_call x3, Pallas kernels, near(): pl.pallas_call(near_kernel, grid=(count,), in_specs=specs, out_specs=[own...  68.1 us
    pallas_call x1, Pallas kernels, far(): pl.pallas_call(far_kernel, grid=(groups,), in_specs=whole + [block, pl.Bl...  15.7 us
    ppermute x11, starting transfers between devices, swapped(): lax.ppermute(array, axis, [(i, i ^ bits) for i in range(lax.axis_size(axi...  10.7 us
    ppermute x11, waiting for transfers between devices, swapped(): lax.ppermute(array, axis, [(i, i ^ bits) for i in range(lax.axis_size(axi...  9.47 us
    ppermute x3, starting transfers between devices, local(): lax.ppermute(squares, 'head', [(i, (i + s) % 4) for i in range(4)])  6.54 us
    pallas_call x1, Pallas kernels, normed(): pl.pallas_call(functools.partial(norm_kernel, features), grid=(groups,),...  4.76 us
    unnamed x9, local copies, waits for them, and re-layouts  4.41 us
    pallas_call x1, Pallas kernels, pool(): pl.pallas_call(pool_kernel, grid=(groups,), in_specs=[block, block], out_...  3.95 us
  transfers between devices with their start and end apart: 14, of which 6 were waited for; matrix products, arithmetic and copies ran while one was open for 0% of the time, Pallas kernels for 54%

commit v1 on v0

v1 whole, which is shorter than its diff:
```python
import functools
import math

import jax
import jax.numpy as jnp
from jax import lax
from jax.experimental import pallas as pl
from jax.experimental.pallas import tpu as pltpu
from jax.sharding import PartitionSpec as P

HEAD_DIM = 128
BLOCK = 128
GROUP = 256
LOG2_SCALE = math.log2(math.e) / math.sqrt(HEAD_DIM)
F32 = jnp.float32
BF16 = jnp.bfloat16
NT = (((1,), (1,)), ((), ()))
MIB = 1 << 20


def iota2(shape, dim):
    return lax.broadcasted_iota(jnp.int32, shape, dim)


def averaging(levels, width):
    parts = []
    for level in levels:
        shape = (width >> level, width)
        hit = (iota2(shape, 1) >> level) == iota2(shape, 0)
        parts.append(jnp.where(hit, 2.0**-level, 0.0))
    return jnp.concatenate(parts, axis=0).astype(BF16)


def slab_order(rows, slabs):
    shape = (rows, rows)
    per = rows // slabs
    row = iota2(shape, 0)
    source = (row % per) * slabs + row // per
    return jnp.where(iota2(shape, 1) == source, 1.0, 0.0).astype(BF16)


def twice(array, per):
    count, width = array.shape[0] // per, array.shape[1]
    wide = jnp.broadcast_to(array.reshape(count, 1, per, width), (count, 2, per, width))
    return wide.reshape(2 * count * per, width)


def halve_slabs(array, per):
    count, width = array.shape[0] // (2 * per), array.shape[1]
    pairs = array.reshape(count, 2, per, width)
    return ((pairs[:, 0] + pairs[:, 1]) * 0.5).reshape(count * per, width)


def score_all(queries, keys):
    return [lax.dot_general(q, k, NT, preferred_element_type=F32) for q, k in zip(queries, keys)]


def weigh_all(scores, per):
    results, peak = [], None
    for index, level in enumerate(scores):
        own, scale = jnp.max(level, axis=1, keepdims=True), None
        if peak is not None:
            coarse = twice(peak, per)
            own = jnp.maximum(own, coarse)
            scale = 2.0 * jnp.exp2((coarse - own) * LOG2_SCALE)
        peak = own
        weights = jnp.exp2((level - peak) * LOG2_SCALE)
        norm = None if index + 1 == len(scores) else jnp.sum(weights, axis=1, keepdims=True)
        results.append((weights.astype(BF16), norm, scale))
    return results, peak


def sum_all(results, values, per):
    norm = value = None
    for index, ((weights, total, scale), v) in enumerate(zip(results, values)):
        if total is None:
            v = jnp.concatenate([v, jnp.ones_like(v)], axis=1)
        summed = jnp.dot(weights, v, preferred_element_type=F32)
        if total is None:
            summed, total = summed[:, :HEAD_DIM], summed[:, HEAD_DIM:]
        if scale is not None:
            total = total + scale * twice(norm, per)
            summed = summed + scale * twice(value, per)
        norm, value = total, summed
    return norm, value


def pool_kernel(
    k_hbm, v_hbm, k0, v0, k1, v1, k2, v2, k3, v3, kv4, kv5, kv6, kv7, kv8, sems
):
    groups = k0.shape[0] // GROUP
    sides = ((k_hbm, k0, k1, k2, k3), (v_hbm, v0, v1, v2, v3))

    def copy(index, group):
        rows = pl.ds(group * GROUP, GROUP)
        return pltpu.make_async_copy(sides[index][0].at[rows], sides[index][1].at[rows], sems.at[index, group])

    for group in range(groups):
        for index in range(2):
            copy(index, group).start()
    matrix = jnp.concatenate([averaging((1, 2, 3, 4), GROUP), jnp.zeros((16, GROUP), BF16)], axis=0)
    for group in range(groups):
        for index, (_, o0, o1, o2, o3) in enumerate(sides):
            copy(index, group).wait()
            rows = o0[group * GROUP : (group + 1) * GROUP]
            pooled = jnp.dot(matrix, rows, preferred_element_type=F32).astype(BF16)
            o1[group * 128 : group * 128 + 128] = pooled[:128]
            o2[group * 64 : group * 64 + 64] = pooled[128:192]
            o3[group * 32 : group * 32 + 32] = pooled[192:224]
            kv4[index, group * 16 : group * 16 + 16] = pooled[224:240]
    matrix = jnp.concatenate([averaging((1, 2, 3, 4), BLOCK), jnp.zeros((8, BLOCK), BF16)], axis=0)
    for index in range(2):
        pooled = jnp.dot(matrix, kv4[index], preferred_element_type=F32).astype(BF16)
        kv5[index] = pooled[:64]
        kv6[index] = pooled[64:96]
        kv7[index] = pooled[96:112]
        kv8[index] = pooled[112:128]


def pool(keys, values):
    rows, width = keys.shape
    shapes = [pltpu.VMEM((rows >> level, width), BF16) for level in range(4) for _ in range(2)]
    shapes += [jax.ShapeDtypeStruct((2, count, width), BF16) for count in (128, 64, 32, 16, 16)]
    return pl.pallas_call(
        pool_kernel,
        in_specs=[pl.BlockSpec(memory_space=pl.ANY)] * 2,
        out_specs=[pl.BlockSpec(memory_space=pltpu.VMEM)] * len(shapes),
        out_shape=shapes,
        scratch_shapes=[pltpu.SemaphoreType.DMA((2, rows // GROUP))],
        compiler_params=pltpu.CompilerParams(vmem_limit_bytes=28 * MIB),
        cost_estimate=pl.CostEstimate(flops=2 * 2 * rows * GROUP * width, bytes_accessed=8 * MIB, transcendentals=0),
        name="pool",
    )(pltpu.with_memory_space_constraint(keys, pltpu.HBM), pltpu.with_memory_space_constraint(values, pltpu.HBM))


def near_kernel(start, q_ref, k0, v0, k1, v1, k2, v2, k3, v3, att_ref, log_ref, q4_ref):
    perm = slab_order(GROUP, 16)
    heads = [slice(c, c + HEAD_DIM) for c in range(0, q_ref.shape[1], HEAD_DIM)]
    lane = iota2((GROUP, HEAD_DIM), 1)

    def at(index, count):
        return pl.ds(pl.multiple_of(index * count, count), count)

    @pl.loop(0, att_ref.shape[0] // GROUP)
    def _(step):
        group = start + step
        level = jnp.dot(perm, q_ref[at(group, GROUP), :], preferred_element_type=F32)
        queries = [level.astype(BF16)]
        for _ in range(4):
            queries.insert(0, halve_slabs(level, 16).astype(BF16))
            level = queries[0].astype(F32)
        q4_ref[at(step, 16), :] = queries.pop(0)
        places = [at((group >> level) ^ 1, BLOCK) for level in (2, 1, 0)] + [at(group, GROUP)]
        keys, values = (
            [[ref[place, cols] for ref, place in zip(refs, places)] for cols in heads]
            for refs in ((k3, k2, k1, k0), (v3, v2, v1, v0))
        )
        scores = [score_all([q[:, cols] for q in queries], keys[head]) for head, cols in enumerate(heads)]
        weighed = [weigh_all(levels, 16) for levels in scores]
        logs = jnp.zeros((GROUP, HEAD_DIM), F32)
        for head, cols in enumerate(heads):
            results, peak = weighed[head]
            norm, value = sum_all(results, values[head], 16)
            att_ref[at(step, GROUP), cols] = (value * (1.0 / norm)).astype(BF16)
            logs = jnp.where(lane == head, peak * LOG2_SCALE + jnp.log2(norm), logs)
        log_ref[at(step, GROUP), :] = logs


def near(queries, pooled, start, count):
    width = queries.shape[1]
    return pl.pallas_call(
        functools.partial(near_kernel, start),
        in_specs=[pl.BlockSpec(memory_space=pltpu.VMEM)] * 9,
        out_specs=[pl.BlockSpec(memory_space=pltpu.VMEM)] * 3,
        out_shape=[
            pltpu.VMEM((count * GROUP, width), BF16),
            pltpu.VMEM((count * GROUP, HEAD_DIM), F32),
            pltpu.VMEM((count * 16, width), BF16),
        ],
        compiler_params=pltpu.CompilerParams(vmem_limit_bytes=28 * MIB),
        cost_estimate=pl.CostEstimate(
            flops=count * 8 * 2 * 2 * GROUP * GROUP * 256, bytes_accessed=count * 3 * MIB, transcendentals=count * 8 * 98304
        ),
        name="near",
    )(queries, *pooled)


def far_kernel(s4, x_own, y2_own, y4_own, y6_own, x_far, y2_far, y4_far, y6_far, *rest):
    parts, (att_ref, sq_ref, coarse, coarse_log) = rest[:-4], rest[-4:]
    near_refs, log_refs, q4_refs = parts[0::3], parts[1::3], parts[2::3]
    heads = [slice(c, c + HEAD_DIM) for c in range(0, att_ref.shape[1], HEAD_DIM)]

    def coarse_levels():
        q4 = jnp.concatenate([ref[...] for ref in q4_refs], axis=0)
        level = jnp.dot(slab_order(BLOCK, 16), q4, preferred_element_type=F32)
        queries = [level.astype(BF16)]
        for _ in range(4):
            queries.insert(0, halve_slabs(level, 8).astype(BF16))
            level = queries[0].astype(F32)
        sides = ((x_own, y2_own, y4_own, y6_own), (x_far, y2_far, y4_far, y6_far))
        pieces = [[], [], [], [], [(s4, 0, 128)]]
        for x, y2, y4, y6 in sides:
            pieces[0] += [(x, 16, 32), (y2, 80, 96), (y4, 48, 64), (y6, 48, 64)]
            pieces[1] += [(x, 0, 16), (y2, 64, 80), (y4, 32, 48), (y6, 32, 48)]
            pieces[2] += [(y4, 0, 32), (y6, 0, 32)]
            pieces[3] += [(y2, 0, 64)]
        keys, values = (
            [jnp.concatenate([ref[part, lo:hi, :] for ref, lo, hi in level], axis=0) for level in pieces]
            for part in (0, 1)
        )
        scores = [score_all([q[:, cols] for q in queries], [k[:, cols] for k in keys]) for cols in heads]
        weighed = [weigh_all(levels, 8) for levels in scores]
        lane = iota2((BLOCK, HEAD_DIM), 1)
        logs = jnp.zeros((BLOCK, HEAD_DIM), F32)
        for head, cols in enumerate(heads):
            results, peak = weighed[head]
            norm, value = sum_all(results, [v[:, cols] for v in values], 8)
            value = value * (1.0 / norm)
            for slab in range(16):
                coarse[head, pl.ds(slab, 8, stride=16), :] = value[slab * 8 : slab * 8 + 8]
            logs = jnp.where(lane == head, peak * LOG2_SCALE + jnp.log2(norm) + 4.0, logs)
        for slab in range(16):
            coarse_log[pl.ds(slab, 8, stride=16), :] = logs[slab * 8 : slab * 8 + 8]

    def merge(near_ref, log_ref, first, step):
        def at(index, count):
            return pl.ds(pl.multiple_of(index * count, count), count)

        group = first + step
        gap = log_ref[at(step, GROUP), :].reshape(16, 16, HEAD_DIM) - coarse_log[at(group, 16), :][None]
        share = (1.0 / (1.0 + jnp.exp2(gap))).reshape(GROUP, HEAD_DIM)
        squares = jnp.zeros((GROUP, HEAD_DIM), F32)
        for head, cols in enumerate(heads):
            part = near_ref[at(step, GROUP), cols].astype(F32)
            delta = (coarse[head, at(group, 16), :][None] - part.reshape(16, 16, HEAD_DIM)).reshape(GROUP, HEAD_DIM)
            attended = part + share[:, head : head + 1] * delta
            squares = squares + attended * attended
            att_ref[at(group, GROUP), cols] = attended.astype(BF16)
        sums = lax.dot_general(
            jnp.ones((8, HEAD_DIM), F32), squares, NT, precision=lax.Precision.HIGHEST, preferred_element_type=F32
        )
        sq_ref[pl.ds(group, 1), :] = sums[:1]

    coarse_levels()
    first = 0
    for near_ref, log_ref in zip(near_refs, log_refs):
        count = near_ref.shape[0] // GROUP

        @pl.loop(0, count)
        def _(step, near_ref=near_ref, log_ref=log_ref, first=first):
            merge(near_ref, log_ref, first, step)

        first += count


def far(s4, own, other, parts):
    operands = [s4, *own, *other, *[array for part in parts for array in part]]
    rows, width = sum(part[0].shape[0] for part in parts), s4.shape[2]
    whole = pl.BlockSpec(memory_space=pltpu.VMEM)
    return pl.pallas_call(
        far_kernel,
        in_specs=[whole] * len(operands),
        out_specs=[whole, whole],
        out_shape=[pltpu.VMEM((rows, width), BF16), jax.ShapeDtypeStruct((rows // GROUP, GROUP), F32)],
        scratch_shapes=[pltpu.VMEM((width // HEAD_DIM, BLOCK, HEAD_DIM), F32), pltpu.VMEM((BLOCK, HEAD_DIM), F32)],
        compiler_params=pltpu.CompilerParams(vmem_limit_bytes=28 * MIB),
        name="far",
    )(*operands)


def norm_kernel(features, att_ref, s0, s1, s2, s3, gain_ref, out_hbm, out_vmem, sems):
    shape = (GROUP, GROUP)
    source = (iota2(shape, 0) % 16) * 16 + iota2(shape, 0) // 16
    hit = iota2(shape, 1) == source
    scale = lax.rsqrt(((s0[...] + s1[...]) + (s2[...] + s3[...])) / features + 1e-06)
    copies = []
    for group in range(att_ref.shape[0] // GROUP):
        rows = pl.ds(group * GROUP, GROUP)
        matrix = jnp.where(hit, scale[group : group + 1], 0.0).astype(BF16)
        mixed = jnp.dot(matrix, att_ref[rows, :], preferred_element_type=F32)
        out_vmem[rows, :] = (mixed * gain_ref[...]).astype(BF16)
        copies.append(pltpu.make_async_copy(out_vmem.at[rows], out_hbm.at[rows], sems.at[group]))
        copies[-1].start()
    for copy in copies:
        copy.wait()


def normed(att, sums, gain, features):
    rows, width = att.shape
    whole = pl.BlockSpec(memory_space=pltpu.VMEM)
    return pl.pallas_call(
        functools.partial(norm_kernel, features),
        in_specs=[whole] * 6,
        out_specs=pl.BlockSpec(memory_space=pl.ANY),
        out_shape=jax.ShapeDtypeStruct((rows, width), BF16),
        scratch_shapes=[pltpu.VMEM((rows, width), BF16), pltpu.SemaphoreType.DMA((rows // GROUP,))],
        compiler_params=pltpu.CompilerParams(vmem_limit_bytes=28 * MIB),
        name="norm",
    )(att, *sums, gain.reshape(1, width))


def swapped(array, axis, bits):
    return lax.ppermute(array, axis, [(i, i ^ bits) for i in range(lax.axis_size(axis))])


def local(queries, keys, values, gain):
    *pooled, kv4, kv5, kv6, kv7, kv8 = pool(keys, values)
    rows8 = kv8[:, :8]
    x7 = swapped(kv7, "seq", 8)
    x8a = swapped(rows8, "seq", 16)
    x8b = swapped(rows8, "seq", 24)
    s4 = swapped(kv4, "seq", 1)
    first = near(queries, pooled, 0, 2)
    x7, x8a, x8b, first = lax.optimization_barrier((x7, x8a, x8b, first))
    x_own = jnp.concatenate([x7, x8a, x8b], axis=1)
    to2 = jnp.concatenate([kv5, x_own], axis=1)
    to46 = jnp.concatenate([kv6, x_own], axis=1)
    own = [x_own, swapped(to2, "seq", 2), swapped(to46, "seq", 4), swapped(to46, "seq", 6)]
    second = near(queries, pooled, 2, 4)
    own, second = lax.optimization_barrier((own, second))
    other = [swapped(a, "seq", 1) for a in own]
    third = near(queries, pooled, 6, 2)
    att, squares = far(s4, own, other, (first, second, third))
    sums = [squares] + [
        lax.ppermute(squares, "head", [(i, (i + s) % 4) for i in range(4)]) for s in (1, 2, 3)
    ]
    return normed(att, sums, gain, lax.axis_size("head") * queries.shape[1])


def solution(mesh):
    return jax.shard_map(
        local,
        mesh=mesh,
        in_specs=(P("seq", "head"), P("seq", "head"), P("seq", "head"), P("head")),
        out_specs=P("seq", "head"),
        check_vma=False,
    )
```

time: 128 us -> 58.7 us (0.46); the launches traced: 126 us -> 58.6 us
  Pallas kernels: 92.5 us -> 31.7 us
  local copies, waits for them, and re-layouts: 4.42 us -> 0.04 us
  waiting for transfers between devices: 12.1 us -> 9.37 us
    pallas_call x6, Pallas kernels: 92.5 us -> 31.7 us  [the longest x3 16.4 us: near(): pl.pallas_call(functools.partial(near_kernel, start), in_specs=[pl.BlockS...]
    unnamed x9 -> x7, local copies, waits for them, and re-layouts: 4.41 us -> 0.03 us
    ppermute x11, waiting for transfers between devices: 9.47 us -> 6.73 us  [swapped(): lax.ppermute(array, axis, [(i, i ^ bits) for i in range(lax.axis_size(axi...]
  transfers between devices with their start and end apart: 14 -> 14, of which waited for: 6 -> 3; matrix products, arithmetic and copies ran while one was open for 0% -> 0% of each run, Pallas kernels for 54% -> 28%
where the time goes in v1:
time: 58.7 us; the launch traced here: 58.6 us
  Pallas kernels  31.7 us (54%)
  starting transfers between devices  17.1 us (29%)
  waiting for transfers between devices  9.37 us (16%)
    pallas_call x3, Pallas kernels, near(): pl.pallas_call(functools.partial(near_kernel, start), in_specs=[pl.BlockS...  16.4 us
    ppermute x11, starting transfers between devices, swapped(): lax.ppermute(array, axis, [(i, i ^ bits) for i in range(lax.axis_size(axi...  10.6 us
    ppermute x11, waiting for transfers between devices, swapped(): lax.ppermute(array, axis, [(i, i ^ bits) for i in range(lax.axis_size(axi...  6.73 us
    pallas_call x1, Pallas kernels, far(): pl.pallas_call(far_kernel, in_specs=[whole] * len(operands), out_specs=[w...  6.59 us
    ppermute x3, starting transfers between devices, local(): lax.ppermute(squares, 'head', [(i, (i + s) % 4) for i in range(4)])  6.53 us
    pallas_call x1, Pallas kernels, pool(): pl.pallas_call(pool_kernel, in_specs=[pl.BlockSpec(memory_space=pl.ANY)]...  6.34 us
    ppermute x3, waiting for transfers between devices, local(): lax.ppermute(squares, 'head', [(i, (i + s) % 4) for i in range(4)])  2.64 us
    pallas_call x1, Pallas kernels, normed(): pl.pallas_call(functools.partial(norm_kernel, features), in_specs=[whole]...  2.38 us
  transfers between devices with their start and end apart: 14, of which 3 were waited for; matrix products, arithmetic and copies ran while one was open for 0% of the time, Pallas kernels for 28%

profile of v1, /device:TPU:2, one launch (start us, length us, event | category | flops | bytes accessed | tf_op | source)
XLA Modules:
  0.0 58.6 jit_solution(16345536555607016646)
XLA Ops:
  0.0 0.0 copy-start
  0.0 6.3 %pool.1 = (bf16[2048,1024]{1,0:T(8,128)(2,1)S(1)}, bf16[2048,1024]{1,0:T(8,128)(2,1)S(1)}, bf16[1024,1024]{1,0:T(8,128)(2,1)S(1)}, bf16[1024,1024]{1,0:T(8,128)(...) custom-call(bf16[2048,1024]{1,0:T(8,128)(2,1)} %k_hbm.1, ...), custom_call_target="tpu_custom_call" | custom-call | flops 2147483648 | bytes 8388608 | tf_op jit(solution)/shard_map/pool/pallas_call | solution.py:124
  6.4 2.2 %collective-permute-start.2 = (bf16[2,8,1024]{2,1,0:T(8,128)(2,1)S(1)}, bf16[2,8,1024]{2,1,0:T(8,128)(2,1)S(1)}, u32[]{:S(2)}, u32[]{:S(2)}) collective-permute-start(bf16[2,8,1024]{2,1,0:T(8,128)(2,1)S(1)} %slice.3), channel_id=1, source_target_pairs={{0,64},{4,68},{8,72},{12,76},{16,80},{20,84},{24,88},{28,92},{32,9... | collective-permute-start | bytes 98312 | tf_op jit(solution)/shard_map/ppermute | solution.py:303
  8.6 0.0 collective-permute-start.3
  8.6 2.6 %collective-permute-start.1 = (bf16[2,16,1024]{2,1,0:T(8,128)(2,1)S(1)}, bf16[2,16,1024]{2,1,0:T(8,128)(2,1)S(1)}, u32[]{:S(2)}, u32[]{:S(2)}) collective-permute-start(bf16[2,16,1024]{2,1,0:T(8,128)(2,1)S(1)} %get-tuple-element.43), channel_id=1, source_target_pairs={{0,32},{4,36},{8,40},{12,44},{16,48},{20,52},{24,56},{28,60},{32,0... | collective-permute-start | bytes 196616 | tf_op jit(solution)/shard_map/ppermute | solution.py:303
  11.1 0.0 collective-permute-start
  11.2 0.0 copy-done
  11.2 4.1 %near.3 = (bf16[512,1024]{1,0:T(8,128)(2,1)S(1)}, f32[512,128]{1,0:T(8,128)S(1)}, bf16[32,1024]{1,0:T(8,128)(2,1)S(1)}) custom-call(bf16[2048,1024]{1,0:T(8,128)(2,1)S(1)} %copy-done, bf16[2048,1024]{1,0:T(8,128)(2,1)S(1)} %get-tuple-element.45.k0, bf16[2048,1024]{1,0:T(8,128)(2,1)S(1)} %get-tuple-element.46.v0, ...), custom_call_target="tpu_custom_call" | custom-call | flops 1073741824 | bytes 6291456 | tf_op jit(solution)/shard_map/near/pallas_call | solution.py:171
  15.3 0.0 collective-permute-done.2
  15.3 0.0 collective-permute-done.3
  15.3 0.0 collective-permute-done.1
  15.4 1.7 %collective-permute-start.4 = (bf16[2,96,1024]{2,1,0:T(8,128)(2,1)S(1)}, bf16[2,96,1024]{2,1,0:T(8,128)(2,1)S(1)}, u32[]{:S(2)}, u32[]{:S(2)}) collective-permute-start(bf16[2,96,1024]{2,1,0:T(8,128)(2,1)S(1)} %pad_maximum_fusion), channel_id=1, source_target_pairs={{0,8},{4,12},{8,0},{12,4},{16,24},{20,28},{24,16},{28,20},{32,40},... | collective-permute-start | bytes 1179656 | tf_op jit(solution)/shard_map/ppermute | solution.py:303
  17.1 2.9 %collective-permute-start.5 = (bf16[2,64,1024]{2,1,0:T(8,128)(2,1)S(1)}, bf16[2,64,1024]{2,1,0:T(8,128)(2,1)S(1)}, u32[]{:S(2)}, u32[]{:S(2)}) collective-permute-start(bf16[2,64,1024]{2,1,0:T(8,128)(2,1)S(1)} %constant_dynamic-update-slice_fusion), channel_id=1, source_target_pairs={{0,16},{4,20},{8,24},{12,28},{16,0},{20,4},{24,8},{28,12},{32,48},... | collective-permute-start | bytes 786440 | tf_op jit(solution)/shard_map/ppermute | solution.py:303
  20.0 0.2 collective-permute-start.6
  20.2 8.2 %near.4 = (bf16[1024,1024]{1,0:T(8,128)(2,1)S(1)}, f32[1024,128]{1,0:T(8,128)S(1)}, bf16[64,1024]{1,0:T(8,128)(2,1)S(1)}) custom-call(bf16[2048,1024]{1,0:T(8,128)(2,1)S(1)} %copy-done, bf16[2048,1024]{1,0:T(8,128)(2,1)S(1)} %get-tuple-element.45.k0, bf16[2048,1024]{1,0:T(8,128)(2,1)S(1)} %get-tuple-element.46.v0, ...), custom_call_target="tpu_custom_call" | custom-call | flops 2147483648 | bytes 12582912 | tf_op jit(solution)/shard_map/near/pallas_call | solution.py:171
  28.4 6.7 %collective-permute-done.5.y4_own = bf16[2,64,1024]{2,1,0:T(8,128)(2,1)S(1)} collective-permute-done((bf16[2,64,1024]{2,1,0:T(8,128)(2,1)S(1)}, bf16[2,64,1024]{2,1,0:T(8,128)(2,1)S(1)}, u32[]{:S(2)}, u32[]{:S(2)}) %collective-permute-start.5) | collective-permute-done | bytes 262176 | tf_op jit(solution)/shard_map/ppermute | solution.py:303
  35.1 0.0 collective-permute-done.6.y6_own
  35.1 0.0 collective-permute-done.4.y2_own
  35.1 0.0 collective-permute-start.8
  35.1 0.5 collective-permute-start.10
  35.6 0.1 collective-permute-start.9
  35.7 0.4 collective-permute-start.7
  36.1 4.1 %near.5 = (bf16[512,1024]{1,0:T(8,128)(2,1)S(1)}, f32[512,128]{1,0:T(8,128)S(1)}, bf16[32,1024]{1,0:T(8,128)(2,1)S(1)}) custom-call(bf16[2048,1024]{1,0:T(8,128)(2,1)S(1)} %copy-done, bf16[2048,1024]{1,0:T(8,128)(2,1)S(1)} %get-tuple-element.45.k0, bf16[2048,1024]{1,0:T(8,128)(2,1)S(1)} %get-tuple-element.46.v0, ...), custom_call_target="tpu_custom_call" | custom-call | flops 1073741824 | bytes 6291456 | tf_op jit(solution)/shard_map/near/pallas_call | solution.py:171
  40.2 0.0 copy-start.1
  40.2 0.0 collective-permute-done.s4
  40.2 0.0 collective-permute-done.7.x_far
  40.2 0.0 collective-permute-done.10.y6_far
  40.3 0.0 collective-permute-done.9.y4_far
  40.3 0.0 collective-permute-done.8.y2_far
  40.3 6.6 %far.1 = (bf16[2048,1024]{1,0:T(8,128)(2,1)S(1)}, f32[8,256]{1,0:T(8,128)S(1)}) custom-call(bf16[2,128,1024]{2,1,0:T(8,128)(2,1)S(1)} %collective-permute-done.s4, bf16[2,32,1024]{2,1,0:T(8,128)(2,1)S(1)} %pad_maximum_fusion.1.x_own, bf16[2,96,1024]{2,1,0:T(8,128)(2,1)S(1)} %collective-permute-done.4.y2_own, ...), custom_call_target="tpu_custom_call" | custom-call | tf_op jit(solution)/shard_map/far/pallas_call | solution.py:260
  46.9 1.9 %collective-permute-start.11 = (f32[8,256]{1,0:T(8,128)S(1)}, f32[8,256]{1,0:T(8,128)S(1)}, u32[]{:S(2)}, u32[]{:S(2)}) collective-permute-start(f32[8,256]{1,0:T(8,128)S(1)} %get-tuple-element.78.s0), channel_id=1, source_target_pairs={{0,1},{1,2},{2,3},{3,0},{4,5},{5,6},{6,7},{7,4},{8,9},{9,10},{10,1... | collective-permute-start | bytes 24584 | tf_op jit(solution)/shard_map/ppermute | solution.py:325
  48.8 3.6 %collective-permute-start.12 = (f32[8,256]{1,0:T(8,128)S(1)}, f32[8,256]{1,0:T(8,128)S(1)}, u32[]{:S(2)}, u32[]{:S(2)}) collective-permute-start(f32[8,256]{1,0:T(8,128)S(1)} %get-tuple-element.78.s0), channel_id=1, source_target_pairs={{0,2},{1,3},{2,0},{3,1},{4,6},{5,7},{6,4},{7,5},{8,10},{9,11},{10,... | collective-permute-start | bytes 24584 | tf_op jit(solution)/shard_map/ppermute | solution.py:325
  52.4 1.0 %collective-permute-start.13 = (f32[8,256]{1,0:T(8,128)S(1)}, f32[8,256]{1,0:T(8,128)S(1)}, u32[]{:S(2)}, u32[]{:S(2)}) collective-permute-start(f32[8,256]{1,0:T(8,128)S(1)} %get-tuple-element.78.s0), channel_id=1, source_target_pairs={{0,3},{1,0},{2,1},{3,2},{4,7},{5,4},{6,5},{7,6},{8,11},{9,8},{10,9... | collective-permute-start | bytes 24584 | tf_op jit(solution)/shard_map/ppermute | solution.py:325
  53.4 0.0 collective-permute-done.11.s1
  53.4 0.7 %collective-permute-done.12.s2 = f32[8,256]{1,0:T(8,128)S(1)} collective-permute-done((f32[8,256]{1,0:T(8,128)S(1)}, f32[8,256]{1,0:T(8,128)S(1)}, u32[]{:S(2)}, u32[]{:S(2)}) %collective-permute-start.12) | collective-permute-done | bytes 8224 | tf_op jit(solution)/shard_map/ppermute | solution.py:325
  54.1 1.9 %collective-permute-done.13.s3 = f32[8,256]{1,0:T(8,128)S(1)} collective-permute-done((f32[8,256]{1,0:T(8,128)S(1)}, f32[8,256]{1,0:T(8,128)S(1)}, u32[]{:S(2)}, u32[]{:S(2)}) %collective-permute-start.13) | collective-permute-done | bytes 8224 | tf_op jit(solution)/shard_map/ppermute | solution.py:325
  56.1 0.0 copy-done.1
  56.1 2.4 %norm.1 = bf16[2048,1024]{1,0:T(8,128)(2,1)} custom-call(bf16[2048,1024]{1,0:T(8,128)(2,1)S(1)} %get-tuple-element.77.att_ref, f32[8,256]{1,0:T(8,128)S(1)} %get-tuple-element.78.s0, f32[8,256]{1,0:T(8,128)S(1)} %collective-permute-done.11.s1, f32[8,256]{1,0:T(8,128)S(1)} %collective-permute-done.12.s2, f32[8,256]{1,0:T(8,128)S(1)} %collective-permute-done.13.s3, ...), custom_call_target="tpu_custom_call" | custom-call | tf_op jit(solution)/shard_map/norm/pallas_call | solution.py:291
  (7 shorter events, 0.1 us)
Async XLA Ops:
  0.0 11.2 %copy-start = (bf16[2048,1024]{1,0:T(8,128)(2,1)S(1)}, bf16[2048,1024]{1,0:T(8,128)(2,1)}, u32[]{:S(2)}) copy-start(bf16[2048,1024]{1,0:T(8,128)(2,1)} %q_ref.5) | copy-start | bytes 12582916
  6.4 8.9 %collective-permute-start.2 = (bf16[2,8,1024]{2,1,0:T(8,128)(2,1)S(1)}, bf16[2,8,1024]{2,1,0:T(8,128)(2,1)S(1)}, u32[]{:S(2)}, u32[]{:S(2)}) collective-permute-start(bf16[2,8,1024]{2,1,0:T(8,128)(2,1)S(1)} %slice.3), channel_id=1, source_target_pairs={{0,64},{4,68},{8,72},{12,76},{16,80},{20,84},{24,88},{28,92},{32,9... | collective-permute-start | bytes 98312 | tf_op jit(solution)/shard_map/ppermute | solution.py:303
  8.6 6.8 %collective-permute-start.3 = (bf16[2,8,1024]{2,1,0:T(8,128)(2,1)S(1)}, bf16[2,8,1024]{2,1,0:T(8,128)(2,1)S(1)}, u32[]{:S(2)}, u32[]{:S(2)}) collective-permute-start(bf16[2,8,1024]{2,1,0:T(8,128)(2,1)S(1)} %slice.3), channel_id=1, source_target_pairs={{0,96},{4,100},{8,104},{12,108},{16,112},{20,116},{24,120},{28,124... | collective-permute-start | bytes 98312 | tf_op jit(solution)/shard_map/ppermute | solution.py:303
  8.6 6.8 %collective-permute-start.1 = (bf16[2,16,1024]{2,1,0:T(8,128)(2,1)S(1)}, bf16[2,16,1024]{2,1,0:T(8,128)(2,1)S(1)}, u32[]{:S(2)}, u32[]{:S(2)}) collective-permute-start(bf16[2,16,1024]{2,1,0:T(8,128)(2,1)S(1)} %get-tuple-element.43), channel_id=1, source_target_pairs={{0,32},{4,36},{8,40},{12,44},{16,48},{20,52},{24,56},{28,60},{32,0... | collective-permute-start | bytes 196616 | tf_op jit(solution)/shard_map/ppermute | solution.py:303
  11.1 29.1 %collective-permute-start = (bf16[2,128,1024]{2,1,0:T(8,128)(2,1)S(1)}, bf16[2,128,1024]{2,1,0:T(8,128)(2,1)S(1)}, u32[]{:S(2)}, u32[]{:S(2)}) collective-permute-start(bf16[2,128,1024]{2,1,0:T(8,128)(2,1)S(1)} %get-tuple-element.42), channel_id=1, source_target_pairs={{0,4},{4,0},{8,12},{12,8},{16,20},{20,16},{24,28},{28,24},{32,36},... | collective-permute-start | bytes 1572872 | tf_op jit(solution)/shard_map/ppermute | solution.py:303
  15.4 19.7 %collective-permute-start.4 = (bf16[2,96,1024]{2,1,0:T(8,128)(2,1)S(1)}, bf16[2,96,1024]{2,1,0:T(8,128)(2,1)S(1)}, u32[]{:S(2)}, u32[]{:S(2)}) collective-permute-start(bf16[2,96,1024]{2,1,0:T(8,128)(2,1)S(1)} %pad_maximum_fusion), channel_id=1, source_target_pairs={{0,8},{4,12},{8,0},{12,4},{16,24},{20,28},{24,16},{28,20},{32,40},... | collective-permute-start | bytes 1179656 | tf_op jit(solution)/shard_map/ppermute | solution.py:303
  17.1 18.0 %collective-permute-start.5 = (bf16[2,64,1024]{2,1,0:T(8,128)(2,1)S(1)}, bf16[2,64,1024]{2,1,0:T(8,128)(2,1)S(1)}, u32[]{:S(2)}, u32[]{:S(2)}) collective-permute-start(bf16[2,64,1024]{2,1,0:T(8,128)(2,1)S(1)} %constant_dynamic-update-slice_fusion), channel_id=1, source_target_pairs={{0,16},{4,20},{8,24},{12,28},{16,0},{20,4},{24,8},{28,12},{32,48},... | collective-permute-start | bytes 786440 | tf_op jit(solution)/shard_map/ppermute | solution.py:303
  20.0 15.1 %collective-permute-start.6 = (bf16[2,64,1024]{2,1,0:T(8,128)(2,1)S(1)}, bf16[2,64,1024]{2,1,0:T(8,128)(2,1)S(1)}, u32[]{:S(2)}, u32[]{:S(2)}) collective-permute-start(bf16[2,64,1024]{2,1,0:T(8,128)(2,1)S(1)} %constant_dynamic-update-slice_fusion), channel_id=1, source_target_pairs={{0,24},{4,28},{8,16},{12,20},{16,8},{20,12},{24,0},{28,4},{32,56},... | collective-permute-start | bytes 786440 | tf_op jit(solution)/shard_map/ppermute | solution.py:303
  35.1 5.2 %collective-permute-start.8 = (bf16[2,96,1024]{2,1,0:T(8,128)(2,1)S(1)}, bf16[2,96,1024]{2,1,0:T(8,128)(2,1)S(1)}, u32[]{:S(2)}, u32[]{:S(2)}) collective-permute-start(bf16[2,96,1024]{2,1,0:T(8,128)(2,1)S(1)} %collective-permute-done.4.y2_own), channel_id=1, source_target_pairs={{0,4},{4,0},{8,12},{12,8},{16,20},{20,16},{24,28},{28,24},{32,36},... | collective-permute-start | bytes 1179656 | tf_op jit(solution)/shard_map/ppermute | solution.py:303
  35.1 5.2 %collective-permute-start.10 = (bf16[2,64,1024]{2,1,0:T(8,128)(2,1)S(1)}, bf16[2,64,1024]{2,1,0:T(8,128)(2,1)S(1)}, u32[]{:S(2)}, u32[]{:S(2)}) collective-permute-start(bf16[2,64,1024]{2,1,0:T(8,128)(2,1)S(1)} %collective-permute-done.6.y6_own), channel_id=1, source_target_pairs={{0,4},{4,0},{8,12},{12,8},{16,20},{20,16},{24,28},{28,24},{32,36},... | collective-permute-start | bytes 786440 | tf_op jit(solution)/shard_map/ppermute | solution.py:303
  35.6 4.7 %collective-permute-start.9 = (bf16[2,64,1024]{2,1,0:T(8,128)(2,1)S(1)}, bf16[2,64,1024]{2,1,0:T(8,128)(2,1)S(1)}, u32[]{:S(2)}, u32[]{:S(2)}) collective-permute-start(bf16[2,64,1024]{2,1,0:T(8,128)(2,1)S(1)} %collective-permute-done.5.y4_own), channel_id=1, source_target_pairs={{0,4},{4,0},{8,12},{12,8},{16,20},{20,16},{24,28},{28,24},{32,36},... | collective-permute-start | bytes 786440 | tf_op jit(solution)/shard_map/ppermute | solution.py:303
  35.7 4.6 %collective-permute-start.7 = (bf16[2,32,1024]{2,1,0:T(8,128)(2,1)S(1)}, bf16[2,32,1024]{2,1,0:T(8,128)(2,1)S(1)}, u32[]{:S(2)}, u32[]{:S(2)}) collective-permute-start(bf16[2,32,1024]{2,1,0:T(8,128)(2,1)S(1)} %pad_maximum_fusion.1.x_own), channel_id=1, source_target_pairs={{0,4},{4,0},{8,12},{12,8},{16,20},{20,16},{24,28},{28,24},{32,36},... | collective-permute-start | bytes 393224 | tf_op jit(solution)/shard_map/ppermute | solution.py:303
  40.2 15.8 %copy-start.1 = (f32[1024]{0:T(1024)S(1)}, f32[1024]{0:T(1024)}, u32[]{:S(2)}) copy-start(f32[1024]{0:T(1024)} %param.7) | copy-start | bytes 12292
  46.9 6.5 %collective-permute-start.11 = (f32[8,256]{1,0:T(8,128)S(1)}, f32[8,256]{1,0:T(8,128)S(1)}, u32[]{:S(2)}, u32[]{:S(2)}) collective-permute-start(f32[8,256]{1,0:T(8,128)S(1)} %get-tuple-element.78.s0), channel_id=1, source_target_pairs={{0,1},{1,2},{2,3},{3,0},{4,5},{5,6},{6,7},{7,4},{8,9},{9,10},{10,1... | collective-permute-start | bytes 24584 | tf_op jit(solution)/shard_map/ppermute | solution.py:325
  48.8 5.3 %collective-permute-start.12 = (f32[8,256]{1,0:T(8,128)S(1)}, f32[8,256]{1,0:T(8,128)S(1)}, u32[]{:S(2)}, u32[]{:S(2)}) collective-permute-start(f32[8,256]{1,0:T(8,128)S(1)} %get-tuple-element.78.s0), channel_id=1, source_target_pairs={{0,2},{1,3},{2,0},{3,1},{4,6},{5,7},{6,4},{7,5},{8,10},{9,11},{10,... | collective-permute-start | bytes 24584 | tf_op jit(solution)/shard_map/ppermute | solution.py:325
  52.4 3.7 %collective-permute-start.13 = (f32[8,256]{1,0:T(8,128)S(1)}, f32[8,256]{1,0:T(8,128)S(1)}, u32[]{:S(2)}, u32[]{:S(2)}) collective-permute-start(f32[8,256]{1,0:T(8,128)S(1)} %get-tuple-element.78.s0), channel_id=1, source_target_pairs={{0,3},{1,0},{2,1},{3,2},{4,7},{5,4},{6,5},{7,6},{8,11},{9,8},{10,9... | collective-permute-start | bytes 24584 | tf_op jit(solution)/shard_map/ppermute | solution.py:325

commit v2 on v1

--- a/solution.py
+++ b/solution.py
@@ -16,6 +16,7 @@
 BF16 = jnp.bfloat16
 NT = (((1,), (1,)), ((), ()))
 MIB = 1 << 20
+SPLIT = (2, 5, 1)
 
 
 def iota2(shape, dim):
@@ -95,13 +96,16 @@
         rows = pl.ds(group * GROUP, GROUP)
         return pltpu.make_async_copy(sides[index][0].at[rows], sides[index][1].at[rows], sems.at[index, group])
 
-    for group in range(groups):
+    ahead = 3
+    for group in range(ahead):
         for index in range(2):
             copy(index, group).start()
     matrix = jnp.concatenate([averaging((1, 2, 3, 4), GROUP), jnp.zeros((16, GROUP), BF16)], axis=0)
     for group in range(groups):
         for index, (_, o0, o1, o2, o3) in enumerate(sides):
             copy(index, group).wait()
+            if group + ahead < groups:
+                copy(index, group + ahead).start()
             rows = o0[group * GROUP : (group + 1) * GROUP]
             pooled = jnp.dot(matrix, rows, preferred_element_type=F32).astype(BF16)
             o1[group * 128 : group * 128 + 128] = pooled[:128]
@@ -185,7 +189,8 @@
     )(queries, *pooled)
 
 
-def far_kernel(s4, x_own, y2_own, y4_own, y6_own, x_far, y2_far, y4_far, y6_far, *rest):
+def far_kernel(s4, *rest):
+    sides, rest = (rest[:5], rest[5:10]), rest[10:]
     parts, (att_ref, sq_ref, coarse, coarse_log) = rest[:-4], rest[-4:]
     near_refs, log_refs, q4_refs = parts[0::3], parts[1::3], parts[2::3]
     heads = [slice(c, c + HEAD_DIM) for c in range(0, att_ref.shape[1], HEAD_DIM)]
@@ -197,13 +202,13 @@
         for _ in range(4):
             queries.insert(0, halve_slabs(level, 8).astype(BF16))
             level = queries[0].astype(F32)
-        sides = ((x_own, y2_own, y4_own, y6_own), (x_far, y2_far, y4_far, y6_far))
         pieces = [[], [], [], [], [(s4, 0, 128)]]
-        for x, y2, y4, y6 in sides:
-            pieces[0] += [(x, 16, 32), (y2, 80, 96), (y4, 48, 64), (y6, 48, 64)]
-            pieces[1] += [(x, 0, 16), (y2, 64, 80), (y4, 32, 48), (y6, 32, 48)]
+        for l5, x_own, y2, y4, y6 in sides:
+            along_x = [(x_own, 0), (y2, 0), (y4, 32), (y6, 32)]
+            pieces[0] += [(ref, lo + 16, lo + 32) for ref, lo in along_x]
+            pieces[1] += [(ref, lo, lo + 16) for ref, lo in along_x]
             pieces[2] += [(y4, 0, 32), (y6, 0, 32)]
-            pieces[3] += [(y2, 0, 64)]
+            pieces[3] += [(l5, 0, 64)]
         keys, values = (
             [jnp.concatenate([ref[part, lo:hi, :] for ref, lo, hi in level], axis=0) for level in pieces]
             for part in (0, 1)
@@ -224,7 +229,7 @@
 
     def merge(near_ref, log_ref, first, step):
         def at(index, count):
-            return pl.ds(pl.multiple_of(index * count, count), count)
+            return slice(index * count, (index + 1) * count)
 
         group = first + step
         gap = log_ref[at(step, GROUP), :].reshape(16, 16, HEAD_DIM) - coarse_log[at(group, 16), :][None]
@@ -236,20 +241,19 @@
             attended = part + share[:, head : head + 1] * delta
             squares = squares + attended * attended
             att_ref[at(group, GROUP), cols] = attended.astype(BF16)
-        sums = lax.dot_general(
-            jnp.ones((8, HEAD_DIM), F32), squares, NT, precision=lax.Precision.HIGHEST, preferred_element_type=F32
-        )
-        sq_ref[pl.ds(group, 1), :] = sums[:1]
+        high = squares.astype(BF16)
+        low = (squares - high.astype(F32)).astype(BF16)
+        ones = jnp.ones((16, 2 * HEAD_DIM), BF16)
+        pair = jnp.concatenate([high, low], axis=1)
+        sums = lax.dot_general(ones, pair, NT, preferred_element_type=F32)
+        sq_ref[group : group + 1] = sums[:1]
 
     coarse_levels()
     first = 0
     for near_ref, log_ref in zip(near_refs, log_refs):
         count = near_ref.shape[0] // GROUP
-
-        @pl.loop(0, count)
-        def _(step, near_ref=near_ref, log_ref=log_ref, first=first):
+        for step in range(count):
             merge(near_ref, log_ref, first, step)
-
         first += count
 
 
@@ -305,22 +309,25 @@
 
 def local(queries, keys, values, gain):
     *pooled, kv4, kv5, kv6, kv7, kv8 = pool(keys, values)
+    queries, kv7, kv8 = lax.optimization_barrier((queries, kv7, kv8))
     rows8 = kv8[:, :8]
     x7 = swapped(kv7, "seq", 8)
     x8a = swapped(rows8, "seq", 16)
     x8b = swapped(rows8, "seq", 24)
+    l5 = swapped(kv5, "seq", 2)
     s4 = swapped(kv4, "seq", 1)
-    first = near(queries, pooled, 0, 2)
+    first = near(queries, pooled, 0, SPLIT[0])
     x7, x8a, x8b, first = lax.optimization_barrier((x7, x8a, x8b, first))
     x_own = jnp.concatenate([x7, x8a, x8b], axis=1)
-    to2 = jnp.concatenate([kv5, x_own], axis=1)
-    to46 = jnp.concatenate([kv6, x_own], axis=1)
-    own = [x_own, swapped(to2, "seq", 2), swapped(to46, "seq", 4), swapped(to46, "seq", 6)]
-    second = near(queries, pooled, 2, 4)
+    both = jnp.concatenate([kv6, x_own], axis=1)
+    early = [l5, x_own]
+    own = [swapped(x_own, "seq", 2), swapped(both, "seq", 4), swapped(both, "seq", 6)]
+    early_other = [swapped(a, "seq", 1) for a in early]
+    second = near(queries, pooled, SPLIT[0], SPLIT[1])
     own, second = lax.optimization_barrier((own, second))
     other = [swapped(a, "seq", 1) for a in own]
-    third = near(queries, pooled, 6, 2)
-    att, squares = far(s4, own, other, (first, second, third))
+    third = near(queries, pooled, SPLIT[0] + SPLIT[1], SPLIT[2])
+    att, squares = far(s4, early + own, early_other + other, (first, second, third))
     sums = [squares] + [
         lax.ppermute(squares, "head", [(i, (i + s) % 4) for i in range(4)]) for s in (1, 2, 3)
     ]

time: 58.7 us -> 52.1 us (0.89); the launches traced: 58.6 us -> 51.3 us
  waiting for transfers between devices: 9.37 us -> 3.37 us
  Pallas kernels: 31.7 us -> 30 us
    ppermute x11 -> x13, waiting for transfers between devices: 6.73 us -> 0.72 us  [swapped(): lax.ppermute(array, axis, [(i, i ^ bits) for i in range(lax.axis_size(axi...]
    pallas_call x1, Pallas kernels: 6.59 us -> 4.89 us  [far(): pl.pallas_call(far_kernel, in_specs=[whole] * len(operands), out_specs=[w...]
    ppermute x11 -> x13, starting transfers between devices: 10.6 us -> 11 us  [swapped(): lax.ppermute(array, axis, [(i, i ^ bits) for i in range(lax.axis_size(axi...]
  transfers between devices with their start and end apart: 14 -> 16, of which waited for: 3 -> 3; matrix products, arithmetic and copies ran while one was open for 0% -> 0% of each run, Pallas kernels for 28% -> 32%
where the time goes in v2:
time: 52.1 us; the launch traced here: 51.3 us
  Pallas kernels  30 us (58%)
  starting transfers between devices  17.6 us (34%)
  waiting for transfers between devices  3.37 us (6%)
    pallas_call x3, Pallas kernels, near(): pl.pallas_call(functools.partial(near_kernel, start), in_specs=[pl.BlockS...  16.4 us
    ppermute x13, starting transfers between devices, swapped(): lax.ppermute(array, axis, [(i, i ^ bits) for i in range(lax.axis_size(axi...  11 us
    ppermute x3, starting transfers between devices, local(): lax.ppermute(squares, 'head', [(i, (i + s) % 4) for i in range(4)])  6.51 us
    pallas_call x1, Pallas kernels, pool(): pl.pallas_call(pool_kernel, in_specs=[pl.BlockSpec(memory_space=pl.ANY)]...  6.34 us
    pallas_call x1, Pallas kernels, far(): pl.pallas_call(far_kernel, in_specs=[whole] * len(operands), out_specs=[w...  4.89 us
    ppermute x3, waiting for transfers between devices, local(): lax.ppermute(squares, 'head', [(i, (i + s) % 4) for i in range(4)])  2.65 us
    pallas_call x1, Pallas kernels, normed(): pl.pallas_call(functools.partial(norm_kernel, features), in_specs=[whole]...  2.38 us
  transfers between devices with their start and end apart: 16, of which 3 were waited for; matrix products, arithmetic and copies ran while one was open for 0% of the time, Pallas kernels for 32%

profile of v2, /device:TPU:2, one launch (start us, length us, event | category | flops | bytes accessed | tf_op | source)
XLA Modules:
  0.0 51.3 jit_solution(10247518491556164570)
XLA Ops:
  0.0 0.0 copy-start
  0.0 6.3 %pool.1 = (bf16[2048,1024]{1,0:T(8,128)(2,1)S(1)}, bf16[2048,1024]{1,0:T(8,128)(2,1)S(1)}, bf16[1024,1024]{1,0:T(8,128)(2,1)S(1)}, bf16[1024,1024]{1,0:T(8,128)(...) custom-call(bf16[2048,1024]{1,0:T(8,128)(2,1)} %k_hbm.1, ...), custom_call_target="tpu_custom_call" | custom-call | flops 2147483648 | bytes 8388608 | tf_op jit(solution)/shard_map/pool/pallas_call | solution.py:128
  6.4 2.2 %collective-permute-start.3 = (bf16[2,8,1024]{2,1,0:T(8,128)(2,1)S(1)}, bf16[2,8,1024]{2,1,0:T(8,128)(2,1)S(1)}, u32[]{:S(2)}, u32[]{:S(2)}) collective-permute-start(bf16[2,8,1024]{2,1,0:T(8,128)(2,1)S(1)} %slice.3), channel_id=1, source_target_pairs={{0,64},{4,68},{8,72},{12,76},{16,80},{20,84},{24,88},{28,92},{32,9... | collective-permute-start | bytes 98312 | tf_op jit(solution)/shard_map/ppermute | solution.py:307
  8.6 0.0 collective-permute-start.4
  8.6 2.6 %collective-permute-start.2 = (bf16[2,16,1024]{2,1,0:T(8,128)(2,1)S(1)}, bf16[2,16,1024]{2,1,0:T(8,128)(2,1)S(1)}, u32[]{:S(2)}, u32[]{:S(2)}) collective-permute-start(bf16[2,16,1024]{2,1,0:T(8,128)(2,1)S(1)} %get-tuple-element.48), channel_id=1, source_target_pairs={{0,32},{4,36},{8,40},{12,44},{16,48},{20,52},{24,56},{28,60},{32,0... | collective-permute-start | bytes 196616 | tf_op jit(solution)/shard_map/ppermute | solution.py:307
  11.1 1.6 %collective-permute-start.1 = (bf16[2,64,1024]{2,1,0:T(8,128)(2,1)S(1)}, bf16[2,64,1024]{2,1,0:T(8,128)(2,1)S(1)}, u32[]{:S(2)}, u32[]{:S(2)}) collective-permute-start(bf16[2,64,1024]{2,1,0:T(8,128)(2,1)S(1)} %get-tuple-element.45), channel_id=1, source_target_pairs={{0,8},{4,12},{8,0},{12,4},{16,24},{20,28},{24,16},{28,20},{32,40},... | collective-permute-start | bytes 786440 | tf_op jit(solution)/shard_map/ppermute | solution.py:307
  12.7 0.0 copy-done
  12.7 4.1 %near.3 = (bf16[512,1024]{1,0:T(8,128)(2,1)S(1)}, f32[512,128]{1,0:T(8,128)S(1)}, bf16[32,1024]{1,0:T(8,128)(2,1)S(1)}) custom-call(bf16[2048,1024]{1,0:T(8,128)(2,1)S(1)} %copy-done, bf16[2048,1024]{1,0:T(8,128)(2,1)S(1)} %get-tuple-element.51.k0, bf16[2048,1024]{1,0:T(8,128)(2,1)S(1)} %get-tuple-element.52.v0, ...), custom_call_target="tpu_custom_call" | custom-call | flops 1073741824 | bytes 6291456 | tf_op jit(solution)/shard_map/near/pallas_call | solution.py:175
  16.9 0.0 collective-permute-done.3
  16.9 0.0 collective-permute-done.4
  16.9 0.0 collective-permute-done.2
  17.0 3.0 %collective-permute-start.6 = (bf16[2,64,1024]{2,1,0:T(8,128)(2,1)S(1)}, bf16[2,64,1024]{2,1,0:T(8,128)(2,1)S(1)}, u32[]{:S(2)}, u32[]{:S(2)}) collective-permute-start(bf16[2,64,1024]{2,1,0:T(8,128)(2,1)S(1)} %get-tuple-element.85), channel_id=1, source_target_pairs={{0,16},{4,20},{8,24},{12,28},{16,0},{20,4},{24,8},{28,12},{32,48},... | collective-permute-start | bytes 786440 | tf_op jit(solution)/shard_map/ppermute | solution.py:307
  19.9 0.2 collective-permute-start.7
  20.2 0.0 collective-permute-start
  20.2 0.4 collective-permute-start.5
  20.5 10.2 %near.4 = (bf16[1280,1024]{1,0:T(8,128)(2,1)S(1)}, f32[1280,128]{1,0:T(8,128)S(1)}, bf16[80,1024]{1,0:T(8,128)(2,1)S(1)}) custom-call(bf16[2048,1024]{1,0:T(8,128)(2,1)S(1)} %copy-done, bf16[2048,1024]{1,0:T(8,128)(2,1)S(1)} %get-tuple-element.51.k0, bf16[2048,1024]{1,0:T(8,128)(2,1)S(1)} %get-tuple-element.52.v0, ...), custom_call_target="tpu_custom_call" | custom-call | flops 2684354560 | bytes 15728640 | tf_op jit(solution)/shard_map/near/pallas_call | solution.py:175
  30.7 0.0 collective-permute-done.5.rest_2_
  30.8 0.3 collective-permute-start.9
  31.1 0.0 collective-permute-done.1.rest_0_
  31.1 0.3 collective-permute-start.8
  31.4 0.0 collective-permute-done.6.rest_3_
  31.4 0.7 %collective-permute-done.7.rest_4_ = bf16[2,64,1024]{2,1,0:T(8,128)(2,1)S(1)} collective-permute-done((bf16[2,64,1024]{2,1,0:T(8,128)(2,1)S(1)}, bf16[2,64,1024]{2,1,0:T(8,128)(2,1)S(1)}, u32[]{:S(2)}, u32[]{:S(2)}) %collective-permute-start.7) | collective-permute-done | bytes 262176 | tf_op jit(solution)/shard_map/ppermute | solution.py:307
  32.0 0.0 collective-permute-start.11
  32.1 0.5 collective-permute-start.12
  32.6 0.0 collective-permute-done.9.rest_6_
  32.6 0.0 collective-permute-start.10
  32.6 2.0 %near.5 = (bf16[256,1024]{1,0:T(8,128)(2,1)S(1)}, f32[256,128]{1,0:T(8,128)S(1)}, bf16[16,1024]{1,0:T(8,128)(2,1)S(1)}) custom-call(bf16[2048,1024]{1,0:T(8,128)(2,1)S(1)} %copy-done, bf16[2048,1024]{1,0:T(8,128)(2,1)S(1)} %get-tuple-element.51.k0, bf16[2048,1024]{1,0:T(8,128)(2,1)S(1)} %get-tuple-element.52.v0, ...), custom_call_target="tpu_custom_call" | custom-call | flops 536870912 | bytes 3145728 | tf_op jit(solution)/shard_map/near/pallas_call | solution.py:175
  34.6 0.0 copy-start.1
  34.6 0.0 collective-permute-done.10.rest_7_
  34.6 0.0 collective-permute-done.8.rest_5_
  34.7 0.0 collective-permute-done.s4
  34.7 0.0 collective-permute-done.11.rest_8_
  34.7 0.0 collective-permute-done.12.rest_9_
  34.7 4.9 %far.1 = (bf16[2048,1024]{1,0:T(8,128)(2,1)S(1)}, f32[8,256]{1,0:T(8,128)S(1)}) custom-call(bf16[2,128,1024]{2,1,0:T(8,128)(2,1)S(1)} %collective-permute-done.s4, bf16[2,64,1024]{2,1,0:T(8,128)(2,1)S(1)} %collective-permute-done.1.rest_0_, bf16[2,32,1024]{2,1,0:T(8,128)(2,1)S(1)} %get-tuple-element.86.rest_1_, ...), custom_call_target="tpu_custom_call" | custom-call | tf_op jit(solution)/shard_map/far/pallas_call | solution.py:264
  39.6 1.9 %collective-permute-start.13 = (f32[8,256]{1,0:T(8,128)S(1)}, f32[8,256]{1,0:T(8,128)S(1)}, u32[]{:S(2)}, u32[]{:S(2)}) collective-permute-start(f32[8,256]{1,0:T(8,128)S(1)} %get-tuple-element.82.s0), channel_id=1, source_target_pairs={{0,1},{1,2},{2,3},{3,0},{4,5},{5,6},{6,7},{7,4},{8,9},{9,10},{10,1... | collective-permute-start | bytes 24584 | tf_op jit(solution)/shard_map/ppermute | solution.py:332
  41.5 3.6 %collective-permute-start.14 = (f32[8,256]{1,0:T(8,128)S(1)}, f32[8,256]{1,0:T(8,128)S(1)}, u32[]{:S(2)}, u32[]{:S(2)}) collective-permute-start(f32[8,256]{1,0:T(8,128)S(1)} %get-tuple-element.82.s0), channel_id=1, source_target_pairs={{0,2},{1,3},{2,0},{3,1},{4,6},{5,7},{6,4},{7,5},{8,10},{9,11},{10,... | collective-permute-start | bytes 24584 | tf_op jit(solution)/shard_map/ppermute | solution.py:332
  45.1 1.0 %collective-permute-start.15 = (f32[8,256]{1,0:T(8,128)S(1)}, f32[8,256]{1,0:T(8,128)S(1)}, u32[]{:S(2)}, u32[]{:S(2)}) collective-permute-start(f32[8,256]{1,0:T(8,128)S(1)} %get-tuple-element.82.s0), channel_id=1, source_target_pairs={{0,3},{1,0},{2,1},{3,2},{4,7},{5,4},{6,5},{7,6},{8,11},{9,8},{10,9... | collective-permute-start | bytes 24584 | tf_op jit(solution)/shard_map/ppermute | solution.py:332
  46.1 0.0 collective-permute-done.13.s1
  46.1 0.7 %collective-permute-done.14.s2 = f32[8,256]{1,0:T(8,128)S(1)} collective-permute-done((f32[8,256]{1,0:T(8,128)S(1)}, f32[8,256]{1,0:T(8,128)S(1)}, u32[]{:S(2)}, u32[]{:S(2)}) %collective-permute-start.14) | collective-permute-done | bytes 8224 | tf_op jit(solution)/shard_map/ppermute | solution.py:332
  46.8 1.9 %collective-permute-done.15.s3 = f32[8,256]{1,0:T(8,128)S(1)} collective-permute-done((f32[8,256]{1,0:T(8,128)S(1)}, f32[8,256]{1,0:T(8,128)S(1)}, u32[]{:S(2)}, u32[]{:S(2)}) %collective-permute-start.15) | collective-permute-done | bytes 8224 | tf_op jit(solution)/shard_map/ppermute | solution.py:332
  48.7 0.0 copy-done.1
  48.7 2.4 %norm.1 = bf16[2048,1024]{1,0:T(8,128)(2,1)} custom-call(bf16[2048,1024]{1,0:T(8,128)(2,1)S(1)} %get-tuple-element.81.att_ref, f32[8,256]{1,0:T(8,128)S(1)} %get-tuple-element.82.s0, f32[8,256]{1,0:T(8,128)S(1)} %collective-permute-done.13.s1, f32[8,256]{1,0:T(8,128)S(1)} %collective-permute-done.14.s2, f32[8,256]{1,0:T(8,128)S(1)} %collective-permute-done.15.s3, ...), custom_call_target="tpu_custom_call" | custom-call | tf_op jit(solution)/shard_map/norm/pallas_call | solution.py:295
  (5 shorter events, 0.0 us)
Async XLA Ops:
  0.0 12.7 %copy-start = (bf16[2048,1024]{1,0:T(8,128)(2,1)S(1)}, bf16[2048,1024]{1,0:T(8,128)(2,1)}, u32[]{:S(2)}) copy-start(bf16[2048,1024]{1,0:T(8,128)(2,1)} %q_ref.2) | copy-start | bytes 12582916
  6.4 10.5 %collective-permute-start.3 = (bf16[2,8,1024]{2,1,0:T(8,128)(2,1)S(1)}, bf16[2,8,1024]{2,1,0:T(8,128)(2,1)S(1)}, u32[]{:S(2)}, u32[]{:S(2)}) collective-permute-start(bf16[2,8,1024]{2,1,0:T(8,128)(2,1)S(1)} %slice.3), channel_id=1, source_target_pairs={{0,64},{4,68},{8,72},{12,76},{16,80},{20,84},{24,88},{28,92},{32,9... | collective-permute-start | bytes 98312 | tf_op jit(solution)/shard_map/ppermute | solution.py:307
  8.6 8.3 %collective-permute-start.4 = (bf16[2,8,1024]{2,1,0:T(8,128)(2,1)S(1)}, bf16[2,8,1024]{2,1,0:T(8,128)(2,1)S(1)}, u32[]{:S(2)}, u32[]{:S(2)}) collective-permute-start(bf16[2,8,1024]{2,1,0:T(8,128)(2,1)S(1)} %slice.3), channel_id=1, source_target_pairs={{0,96},{4,100},{8,104},{12,108},{16,112},{20,116},{24,120},{28,124... | collective-permute-start | bytes 98312 | tf_op jit(solution)/shard_map/ppermute | solution.py:307
  8.6 8.3 %collective-permute-start.2 = (bf16[2,16,1024]{2,1,0:T(8,128)(2,1)S(1)}, bf16[2,16,1024]{2,1,0:T(8,128)(2,1)S(1)}, u32[]{:S(2)}, u32[]{:S(2)}) collective-permute-start(bf16[2,16,1024]{2,1,0:T(8,128)(2,1)S(1)} %get-tuple-element.48), channel_id=1, source_target_pairs={{0,32},{4,36},{8,40},{12,44},{16,48},{20,52},{24,56},{28,60},{32,0... | collective-permute-start | bytes 196616 | tf_op jit(solution)/shard_map/ppermute | solution.py:307
  11.1 19.9 %collective-permute-start.1 = (bf16[2,64,1024]{2,1,0:T(8,128)(2,1)S(1)}, bf16[2,64,1024]{2,1,0:T(8,128)(2,1)S(1)}, u32[]{:S(2)}, u32[]{:S(2)}) collective-permute-start(bf16[2,64,1024]{2,1,0:T(8,128)(2,1)S(1)} %get-tuple-element.45), channel_id=1, source_target_pairs={{0,8},{4,12},{8,0},{12,4},{16,24},{20,28},{24,16},{28,20},{32,40},... | collective-permute-start | bytes 786440 | tf_op jit(solution)/shard_map/ppermute | solution.py:307
  17.0 14.4 %collective-permute-start.6 = (bf16[2,64,1024]{2,1,0:T(8,128)(2,1)S(1)}, bf16[2,64,1024]{2,1,0:T(8,128)(2,1)S(1)}, u32[]{:S(2)}, u32[]{:S(2)}) collective-permute-start(bf16[2,64,1024]{2,1,0:T(8,128)(2,1)S(1)} %get-tuple-element.85), channel_id=1, source_target_pairs={{0,16},{4,20},{8,24},{12,28},{16,0},{20,4},{24,8},{28,12},{32,48},... | collective-permute-start | bytes 786440 | tf_op jit(solution)/shard_map/ppermute | solution.py:307
  19.9 12.1 %collective-permute-start.7 = (bf16[2,64,1024]{2,1,0:T(8,128)(2,1)S(1)}, bf16[2,64,1024]{2,1,0:T(8,128)(2,1)S(1)}, u32[]{:S(2)}, u32[]{:S(2)}) collective-permute-start(bf16[2,64,1024]{2,1,0:T(8,128)(2,1)S(1)} %get-tuple-element.85), channel_id=1, source_target_pairs={{0,24},{4,28},{8,16},{12,20},{16,8},{20,12},{24,0},{28,4},{32,56},... | collective-permute-start | bytes 786440 | tf_op jit(solution)/shard_map/ppermute | solution.py:307
  20.2 14.5 %collective-permute-start = (bf16[2,128,1024]{2,1,0:T(8,128)(2,1)S(1)}, bf16[2,128,1024]{2,1,0:T(8,128)(2,1)S(1)}, u32[]{:S(2)}, u32[]{:S(2)}) collective-permute-start(bf16[2,128,1024]{2,1,0:T(8,128)(2,1)S(1)} %get-tuple-element.44), channel_id=1, source_target_pairs={{0,4},{4,0},{8,12},{12,8},{16,20},{20,16},{24,28},{28,24},{32,36},... | collective-permute-start | bytes 1572872 | tf_op jit(solution)/shard_map/ppermute | solution.py:307
  20.2 10.6 %collective-permute-start.5 = (bf16[2,32,1024]{2,1,0:T(8,128)(2,1)S(1)}, bf16[2,32,1024]{2,1,0:T(8,128)(2,1)S(1)}, u32[]{:S(2)}, u32[]{:S(2)}) collective-permute-start(bf16[2,32,1024]{2,1,0:T(8,128)(2,1)S(1)} %get-tuple-element.86.rest_1_), channel_id=1, source_target_pairs={{0,8},{4,12},{8,0},{12,4},{16,24},{20,28},{24,16},{28,20},{32,40},... | collective-permute-start | bytes 393224 | tf_op jit(solution)/shard_map/ppermute | solution.py:307
  30.8 1.8 %collective-permute-start.9 = (bf16[2,32,1024]{2,1,0:T(8,128)(2,1)S(1)}, bf16[2,32,1024]{2,1,0:T(8,128)(2,1)S(1)}, u32[]{:S(2)}, u32[]{:S(2)}) collective-permute-start(bf16[2,32,1024]{2,1,0:T(8,128)(2,1)S(1)} %get-tuple-element.86.rest_1_), channel_id=1, source_target_pairs={{0,4},{4,0},{8,12},{12,8},{16,20},{20,16},{24,28},{28,24},{32,36},... | collective-permute-start | bytes 393224 | tf_op jit(solution)/shard_map/ppermute | solution.py:307
  31.1 3.6 %collective-permute-start.8 = (bf16[2,64,1024]{2,1,0:T(8,128)(2,1)S(1)}, bf16[2,64,1024]{2,1,0:T(8,128)(2,1)S(1)}, u32[]{:S(2)}, u32[]{:S(2)}) collective-permute-start(bf16[2,64,1024]{2,1,0:T(8,128)(2,1)S(1)} %collective-permute-done.1.rest_0_), channel_id=1, source_target_pairs={{0,4},{4,0},{8,12},{12,8},{16,20},{20,16},{24,28},{28,24},{32,36},... | collective-permute-start | bytes 786440 | tf_op jit(solution)/shard_map/ppermute | solution.py:307
  32.0 2.6 %collective-permute-start.11 = (bf16[2,64,1024]{2,1,0:T(8,128)(2,1)S(1)}, bf16[2,64,1024]{2,1,0:T(8,128)(2,1)S(1)}, u32[]{:S(2)}, u32[]{:S(2)}) collective-permute-start(bf16[2,64,1024]{2,1,0:T(8,128)(2,1)S(1)} %collective-permute-done.6.rest_3_), channel_id=1, source_target_pairs={{0,4},{4,0},{8,12},{12,8},{16,20},{20,16},{24,28},{28,24},{32,36},... | collective-permute-start | bytes 786440 | tf_op jit(solution)/shard_map/ppermute | solution.py:307
  32.1 2.6 %collective-permute-start.12 = (bf16[2,64,1024]{2,1,0:T(8,128)(2,1)S(1)}, bf16[2,64,1024]{2,1,0:T(8,128)(2,1)S(1)}, u32[]{:S(2)}, u32[]{:S(2)}) collective-permute-start(bf16[2,64,1024]{2,1,0:T(8,128)(2,1)S(1)} %collective-permute-done.7.rest_4_), channel_id=1, source_target_pairs={{0,4},{4,0},{8,12},{12,8},{16,20},{20,16},{24,28},{28,24},{32,36},... | collective-permute-start | bytes 786440 | tf_op jit(solution)/shard_map/ppermute | solution.py:307
  32.6 2.1 %collective-permute-start.10 = (bf16[2,32,1024]{2,1,0:T(8,128)(2,1)S(1)}, bf16[2,32,1024]{2,1,0:T(8,128)(2,1)S(1)}, u32[]{:S(2)}, u32[]{:S(2)}) collective-permute-start(bf16[2,32,1024]{2,1,0:T(8,128)(2,1)S(1)} %collective-permute-done.5.rest_2_), channel_id=1, source_target_pairs={{0,4},{4,0},{8,12},{12,8},{16,20},{20,16},{24,28},{28,24},{32,36},... | collective-permute-start | bytes 393224 | tf_op jit(solution)/shard_map/ppermute | solution.py:307
  34.6 14.1 %copy-start.1 = (f32[1024]{0:T(1024)S(1)}, f32[1024]{0:T(1024)}, u32[]{:S(2)}) copy-start(f32[1024]{0:T(1024)} %param.7) | copy-start | bytes 12292
  39.6 6.5 %collective-permute-start.13 = (f32[8,256]{1,0:T(8,128)S(1)}, f32[8,256]{1,0:T(8,128)S(1)}, u32[]{:S(2)}, u32[]{:S(2)}) collective-permute-start(f32[8,256]{1,0:T(8,128)S(1)} %get-tuple-element.82.s0), channel_id=1, source_target_pairs={{0,1},{1,2},{2,3},{3,0},{4,5},{5,6},{6,7},{7,4},{8,9},{9,10},{10,1... | collective-permute-start | bytes 24584 | tf_op jit(solution)/shard_map/ppermute | solution.py:332
  41.5 5.3 %collective-permute-start.14 = (f32[8,256]{1,0:T(8,128)S(1)}, f32[8,256]{1,0:T(8,128)S(1)}, u32[]{:S(2)}, u32[]{:S(2)}) collective-permute-start(f32[8,256]{1,0:T(8,128)S(1)} %get-tuple-element.82.s0), channel_id=1, source_target_pairs={{0,2},{1,3},{2,0},{3,1},{4,6},{5,7},{6,4},{7,5},{8,10},{9,11},{10,... | collective-permute-start | bytes 24584 | tf_op jit(solution)/shard_map/ppermute | solution.py:332
  45.1 3.7 %collective-permute-start.15 = (f32[8,256]{1,0:T(8,128)S(1)}, f32[8,256]{1,0:T(8,128)S(1)}, u32[]{:S(2)}, u32[]{:S(2)}) collective-permute-start(f32[8,256]{1,0:T(8,128)S(1)} %get-tuple-element.82.s0), channel_id=1, source_target_pairs={{0,3},{1,0},{2,1},{3,2},{4,7},{5,4},{6,5},{7,6},{8,11},{9,8},{10,9... | collective-permute-start | bytes 24584 | tf_op jit(solution)/shard_map/ppermute | solution.py:332

commit v3 on v2

--- a/solution.py
+++ b/solution.py
@@ -17,6 +17,7 @@
 NT = (((1,), (1,)), ((), ()))
 MIB = 1 << 20
 SPLIT = (2, 5, 1)
+TOGETHER = 2
 
 
 def iota2(shape, dim):
@@ -96,22 +97,23 @@
         rows = pl.ds(group * GROUP, GROUP)
         return pltpu.make_async_copy(sides[index][0].at[rows], sides[index][1].at[rows], sems.at[index, group])
 
-    ahead = 3
-    for group in range(ahead):
+    for group in range(groups):
         for index in range(2):
             copy(index, group).start()
     matrix = jnp.concatenate([averaging((1, 2, 3, 4), GROUP), jnp.zeros((16, GROUP), BF16)], axis=0)
-    for group in range(groups):
-        for index, (_, o0, o1, o2, o3) in enumerate(sides):
-            copy(index, group).wait()
-            if group + ahead < groups:
-                copy(index, group + ahead).start()
-            rows = o0[group * GROUP : (group + 1) * GROUP]
-            pooled = jnp.dot(matrix, rows, preferred_element_type=F32).astype(BF16)
-            o1[group * 128 : group * 128 + 128] = pooled[:128]
-            o2[group * 64 : group * 64 + 64] = pooled[128:192]
-            o3[group * 32 : group * 32 + 32] = pooled[192:224]
-            kv4[index, group * 16 : group * 16 + 16] = pooled[224:240]
+    for first in range(0, groups, TOGETHER):
+        here = range(first, first + TOGETHER)
+        for group in here:
+            for index in range(2):
+                copy(index, group).wait()
+        for group in here:
+            for index, (_, o0, o1, o2, o3) in enumerate(sides):
+                rows = o0[group * GROUP : (group + 1) * GROUP]
+                pooled = jnp.dot(matrix, rows, preferred_element_type=F32).astype(BF16)
+                o1[group * 128 : group * 128 + 128] = pooled[:128]
+                o2[group * 64 : group * 64 + 64] = pooled[128:192]
+                o3[group * 32 : group * 32 + 32] = pooled[192:224]
+                kv4[index, group * 16 : group * 16 + 16] = pooled[224:240]
     matrix = jnp.concatenate([averaging((1, 2, 3, 4), BLOCK), jnp.zeros((8, BLOCK), BF16)], axis=0)
     for index in range(2):
         pooled = jnp.dot(matrix, kv4[index], preferred_element_type=F32).astype(BF16)

time: 52.1 us -> 50.6 us (0.971)
  Pallas kernels: 30 us -> 28.5 us
    pallas_call x1, Pallas kernels: 6.34 us -> 4.83 us  [pool(): pl.pallas_call(pool_kernel, in_specs=[pl.BlockSpec(memory_space=pl.ANY)]...]
  transfers between devices with their start and end apart: 16 -> 16, of which waited for: 3 -> 3; matrix products, arithmetic and copies ran while one was open for 0% -> 0% of each run, Pallas kernels for 32% -> 33%
where the time goes in v3:
time: 50.6 us; the launch traced here: 49.8 us
  Pallas kernels  28.5 us (56%)
  starting transfers between devices  17.6 us (35%)
  waiting for transfers between devices  3.35 us (7%)
    pallas_call x3, Pallas kernels, near(): pl.pallas_call(functools.partial(near_kernel, start), in_specs=[pl.BlockS...  16.4 us
    ppermute x13, starting transfers between devices, swapped(): lax.ppermute(array, axis, [(i, i ^ bits) for i in range(lax.axis_size(axi...  11 us
    ppermute x3, starting transfers between devices, local(): lax.ppermute(squares, 'head', [(i, (i + s) % 4) for i in range(4)])  6.52 us
    pallas_call x1, Pallas kernels, far(): pl.pallas_call(far_kernel, in_specs=[whole] * len(operands), out_specs=[w...  4.89 us
    pallas_call x1, Pallas kernels, pool(): pl.pallas_call(pool_kernel, in_specs=[pl.BlockSpec(memory_space=pl.ANY)]...  4.83 us
    ppermute x3, waiting for transfers between devices, local(): lax.ppermute(squares, 'head', [(i, (i + s) % 4) for i in range(4)])  2.64 us
    pallas_call x1, Pallas kernels, normed(): pl.pallas_call(functools.partial(norm_kernel, features), in_specs=[whole]...  2.38 us
  transfers between devices with their start and end apart: 16, of which 3 were waited for; matrix products, arithmetic and copies ran while one was open for 0% of the time, Pallas kernels for 33%

profile of v3, /device:TPU:2, one launch (start us, length us, event | category | flops | bytes accessed | tf_op | source)
XLA Modules:
  0.0 49.8 jit_solution(10920180884251233155)
XLA Ops:
  0.0 0.0 copy-start
  0.0 4.8 %pool.1 = (bf16[2048,1024]{1,0:T(8,128)(2,1)S(1)}, bf16[2048,1024]{1,0:T(8,128)(2,1)S(1)}, bf16[1024,1024]{1,0:T(8,128)(2,1)S(1)}, bf16[1024,1024]{1,0:T(8,128)(...) custom-call(bf16[2048,1024]{1,0:T(8,128)(2,1)} %k_hbm.1, ...), custom_call_target="tpu_custom_call" | custom-call | flops 2147483648 | bytes 8388608 | tf_op jit(solution)/shard_map/pool/pallas_call | solution.py:130
  4.8 2.2 %collective-permute-start.3 = (bf16[2,8,1024]{2,1,0:T(8,128)(2,1)S(1)}, bf16[2,8,1024]{2,1,0:T(8,128)(2,1)S(1)}, u32[]{:S(2)}, u32[]{:S(2)}) collective-permute-start(bf16[2,8,1024]{2,1,0:T(8,128)(2,1)S(1)} %slice.3), channel_id=1, source_target_pairs={{0,64},{4,68},{8,72},{12,76},{16,80},{20,84},{24,88},{28,92},{32,9... | collective-permute-start | bytes 98312 | tf_op jit(solution)/shard_map/ppermute | solution.py:309
  7.1 0.0 collective-permute-start.4
  7.1 2.6 %collective-permute-start.2 = (bf16[2,16,1024]{2,1,0:T(8,128)(2,1)S(1)}, bf16[2,16,1024]{2,1,0:T(8,128)(2,1)S(1)}, u32[]{:S(2)}, u32[]{:S(2)}) collective-permute-start(bf16[2,16,1024]{2,1,0:T(8,128)(2,1)S(1)} %get-tuple-element.48), channel_id=1, source_target_pairs={{0,32},{4,36},{8,40},{12,44},{16,48},{20,52},{24,56},{28,60},{32,0... | collective-permute-start | bytes 196616 | tf_op jit(solution)/shard_map/ppermute | solution.py:309
  9.6 1.6 %collective-permute-start.1 = (bf16[2,64,1024]{2,1,0:T(8,128)(2,1)S(1)}, bf16[2,64,1024]{2,1,0:T(8,128)(2,1)S(1)}, u32[]{:S(2)}, u32[]{:S(2)}) collective-permute-start(bf16[2,64,1024]{2,1,0:T(8,128)(2,1)S(1)} %get-tuple-element.45), channel_id=1, source_target_pairs={{0,8},{4,12},{8,0},{12,4},{16,24},{20,28},{24,16},{28,20},{32,40},... | collective-permute-start | bytes 786440 | tf_op jit(solution)/shard_map/ppermute | solution.py:309
  11.2 0.0 copy-done
  11.2 4.1 %near.3 = (bf16[512,1024]{1,0:T(8,128)(2,1)S(1)}, f32[512,128]{1,0:T(8,128)S(1)}, bf16[32,1024]{1,0:T(8,128)(2,1)S(1)}) custom-call(bf16[2048,1024]{1,0:T(8,128)(2,1)S(1)} %copy-done, bf16[2048,1024]{1,0:T(8,128)(2,1)S(1)} %get-tuple-element.51.k0, bf16[2048,1024]{1,0:T(8,128)(2,1)S(1)} %get-tuple-element.52.v0, ...), custom_call_target="tpu_custom_call" | custom-call | flops 1073741824 | bytes 6291456 | tf_op jit(solution)/shard_map/near/pallas_call | solution.py:177
  15.4 0.0 collective-permute-done.3
  15.4 0.0 collective-permute-done.4
  15.4 0.0 collective-permute-done.2
  15.5 3.0 %collective-permute-start.6 = (bf16[2,64,1024]{2,1,0:T(8,128)(2,1)S(1)}, bf16[2,64,1024]{2,1,0:T(8,128)(2,1)S(1)}, u32[]{:S(2)}, u32[]{:S(2)}) collective-permute-start(bf16[2,64,1024]{2,1,0:T(8,128)(2,1)S(1)} %get-tuple-element.85), channel_id=1, source_target_pairs={{0,16},{4,20},{8,24},{12,28},{16,0},{20,4},{24,8},{28,12},{32,48},... | collective-permute-start | bytes 786440 | tf_op jit(solution)/shard_map/ppermute | solution.py:309
  18.4 0.2 collective-permute-start.7
  18.7 0.0 collective-permute-start
  18.7 0.4 collective-permute-start.5
  19.0 10.2 %near.4 = (bf16[1280,1024]{1,0:T(8,128)(2,1)S(1)}, f32[1280,128]{1,0:T(8,128)S(1)}, bf16[80,1024]{1,0:T(8,128)(2,1)S(1)}) custom-call(bf16[2048,1024]{1,0:T(8,128)(2,1)S(1)} %copy-done, bf16[2048,1024]{1,0:T(8,128)(2,1)S(1)} %get-tuple-element.51.k0, bf16[2048,1024]{1,0:T(8,128)(2,1)S(1)} %get-tuple-element.52.v0, ...), custom_call_target="tpu_custom_call" | custom-call | flops 2684354560 | bytes 15728640 | tf_op jit(solution)/shard_map/near/pallas_call | solution.py:177
  29.2 0.0 collective-permute-done.5.rest_2_
  29.2 0.3 collective-permute-start.9
  29.5 0.0 collective-permute-done.1.rest_0_
  29.6 0.3 collective-permute-start.8
  29.8 0.0 collective-permute-done.6.rest_3_
  29.8 0.7 %collective-permute-done.7.rest_4_ = bf16[2,64,1024]{2,1,0:T(8,128)(2,1)S(1)} collective-permute-done((bf16[2,64,1024]{2,1,0:T(8,128)(2,1)S(1)}, bf16[2,64,1024]{2,1,0:T(8,128)(2,1)S(1)}, u32[]{:S(2)}, u32[]{:S(2)}) %collective-permute-start.7) | collective-permute-done | bytes 262176 | tf_op jit(solution)/shard_map/ppermute | solution.py:309
  30.5 0.0 collective-permute-start.11
  30.5 0.5 collective-permute-start.12
  31.0 0.0 collective-permute-done.9.rest_6_
  31.0 0.0 collective-permute-start.10
  31.1 2.0 %near.5 = (bf16[256,1024]{1,0:T(8,128)(2,1)S(1)}, f32[256,128]{1,0:T(8,128)S(1)}, bf16[16,1024]{1,0:T(8,128)(2,1)S(1)}) custom-call(bf16[2048,1024]{1,0:T(8,128)(2,1)S(1)} %copy-done, bf16[2048,1024]{1,0:T(8,128)(2,1)S(1)} %get-tuple-element.51.k0, bf16[2048,1024]{1,0:T(8,128)(2,1)S(1)} %get-tuple-element.52.v0, ...), custom_call_target="tpu_custom_call" | custom-call | flops 536870912 | bytes 3145728 | tf_op jit(solution)/shard_map/near/pallas_call | solution.py:177
  33.1 0.0 copy-start.1
  33.1 0.0 collective-permute-done.10.rest_7_
  33.1 0.0 collective-permute-done.8.rest_5_
  33.1 0.0 collective-permute-done.s4
  33.2 0.0 collective-permute-done.11.rest_8_
  33.2 0.0 collective-permute-done.12.rest_9_
  33.2 4.9 %far.1 = (bf16[2048,1024]{1,0:T(8,128)(2,1)S(1)}, f32[8,256]{1,0:T(8,128)S(1)}) custom-call(bf16[2,128,1024]{2,1,0:T(8,128)(2,1)S(1)} %collective-permute-done.s4, bf16[2,64,1024]{2,1,0:T(8,128)(2,1)S(1)} %collective-permute-done.1.rest_0_, bf16[2,32,1024]{2,1,0:T(8,128)(2,1)S(1)} %get-tuple-element.86.rest_1_, ...), custom_call_target="tpu_custom_call" | custom-call | tf_op jit(solution)/shard_map/far/pallas_call | solution.py:266
  38.1 1.9 %collective-permute-start.13 = (f32[8,256]{1,0:T(8,128)S(1)}, f32[8,256]{1,0:T(8,128)S(1)}, u32[]{:S(2)}, u32[]{:S(2)}) collective-permute-start(f32[8,256]{1,0:T(8,128)S(1)} %get-tuple-element.82.s0), channel_id=1, source_target_pairs={{0,1},{1,2},{2,3},{3,0},{4,5},{5,6},{6,7},{7,4},{8,9},{9,10},{10,1... | collective-permute-start | bytes 24584 | tf_op jit(solution)/shard_map/ppermute | solution.py:334
  40.0 3.6 %collective-permute-start.14 = (f32[8,256]{1,0:T(8,128)S(1)}, f32[8,256]{1,0:T(8,128)S(1)}, u32[]{:S(2)}, u32[]{:S(2)}) collective-permute-start(f32[8,256]{1,0:T(8,128)S(1)} %get-tuple-element.82.s0), channel_id=1, source_target_pairs={{0,2},{1,3},{2,0},{3,1},{4,6},{5,7},{6,4},{7,5},{8,10},{9,11},{10,... | collective-permute-start | bytes 24584 | tf_op jit(solution)/shard_map/ppermute | solution.py:334
  43.6 1.0 %collective-permute-start.15 = (f32[8,256]{1,0:T(8,128)S(1)}, f32[8,256]{1,0:T(8,128)S(1)}, u32[]{:S(2)}, u32[]{:S(2)}) collective-permute-start(f32[8,256]{1,0:T(8,128)S(1)} %get-tuple-element.82.s0), channel_id=1, source_target_pairs={{0,3},{1,0},{2,1},{3,2},{4,7},{5,4},{6,5},{7,6},{8,11},{9,8},{10,9... | collective-permute-start | bytes 24584 | tf_op jit(solution)/shard_map/ppermute | solution.py:334
  44.6 0.0 collective-permute-done.13.s1
  44.6 0.7 %collective-permute-done.14.s2 = f32[8,256]{1,0:T(8,128)S(1)} collective-permute-done((f32[8,256]{1,0:T(8,128)S(1)}, f32[8,256]{1,0:T(8,128)S(1)}, u32[]{:S(2)}, u32[]{:S(2)}) %collective-permute-start.14) | collective-permute-done | bytes 8224 | tf_op jit(solution)/shard_map/ppermute | solution.py:334
  45.3 1.9 %collective-permute-done.15.s3 = f32[8,256]{1,0:T(8,128)S(1)} collective-permute-done((f32[8,256]{1,0:T(8,128)S(1)}, f32[8,256]{1,0:T(8,128)S(1)}, u32[]{:S(2)}, u32[]{:S(2)}) %collective-permute-start.15) | collective-permute-done | bytes 8224 | tf_op jit(solution)/shard_map/ppermute | solution.py:334
  47.2 0.0 copy-done.1
  47.2 2.4 %norm.1 = bf16[2048,1024]{1,0:T(8,128)(2,1)} custom-call(bf16[2048,1024]{1,0:T(8,128)(2,1)S(1)} %get-tuple-element.81.att_ref, f32[8,256]{1,0:T(8,128)S(1)} %get-tuple-element.82.s0, f32[8,256]{1,0:T(8,128)S(1)} %collective-permute-done.13.s1, f32[8,256]{1,0:T(8,128)S(1)} %collective-permute-done.14.s2, f32[8,256]{1,0:T(8,128)S(1)} %collective-permute-done.15.s3, ...), custom_call_target="tpu_custom_call" | custom-call | tf_op jit(solution)/shard_map/norm/pallas_call | solution.py:297
  (5 shorter events, 0.0 us)
Async XLA Ops:
  0.0 11.2 %copy-start = (bf16[2048,1024]{1,0:T(8,128)(2,1)S(1)}, bf16[2048,1024]{1,0:T(8,128)(2,1)}, u32[]{:S(2)}) copy-start(bf16[2048,1024]{1,0:T(8,128)(2,1)} %q_ref.2) | copy-start | bytes 12582916
  4.8 10.5 %collective-permute-start.3 = (bf16[2,8,1024]{2,1,0:T(8,128)(2,1)S(1)}, bf16[2,8,1024]{2,1,0:T(8,128)(2,1)S(1)}, u32[]{:S(2)}, u32[]{:S(2)}) collective-permute-start(bf16[2,8,1024]{2,1,0:T(8,128)(2,1)S(1)} %slice.3), channel_id=1, source_target_pairs={{0,64},{4,68},{8,72},{12,76},{16,80},{20,84},{24,88},{28,92},{32,9... | collective-permute-start | bytes 98312 | tf_op jit(solution)/shard_map/ppermute | solution.py:309
  7.1 8.3 %collective-permute-start.4 = (bf16[2,8,1024]{2,1,0:T(8,128)(2,1)S(1)}, bf16[2,8,1024]{2,1,0:T(8,128)(2,1)S(1)}, u32[]{:S(2)}, u32[]{:S(2)}) collective-permute-start(bf16[2,8,1024]{2,1,0:T(8,128)(2,1)S(1)} %slice.3), channel_id=1, source_target_pairs={{0,96},{4,100},{8,104},{12,108},{16,112},{20,116},{24,120},{28,124... | collective-permute-start | bytes 98312 | tf_op jit(solution)/shard_map/ppermute | solution.py:309
  7.1 8.3 %collective-permute-start.2 = (bf16[2,16,1024]{2,1,0:T(8,128)(2,1)S(1)}, bf16[2,16,1024]{2,1,0:T(8,128)(2,1)S(1)}, u32[]{:S(2)}, u32[]{:S(2)}) collective-permute-start(bf16[2,16,1024]{2,1,0:T(8,128)(2,1)S(1)} %get-tuple-element.48), channel_id=1, source_target_pairs={{0,32},{4,36},{8,40},{12,44},{16,48},{20,52},{24,56},{28,60},{32,0... | collective-permute-start | bytes 196616 | tf_op jit(solution)/shard_map/ppermute | solution.py:309
  9.6 19.9 %collective-permute-start.1 = (bf16[2,64,1024]{2,1,0:T(8,128)(2,1)S(1)}, bf16[2,64,1024]{2,1,0:T(8,128)(2,1)S(1)}, u32[]{:S(2)}, u32[]{:S(2)}) collective-permute-start(bf16[2,64,1024]{2,1,0:T(8,128)(2,1)S(1)} %get-tuple-element.45), channel_id=1, source_target_pairs={{0,8},{4,12},{8,0},{12,4},{16,24},{20,28},{24,16},{28,20},{32,40},... | collective-permute-start | bytes 786440 | tf_op jit(solution)/shard_map/ppermute | solution.py:309
  15.5 14.4 %collective-permute-start.6 = (bf16[2,64,1024]{2,1,0:T(8,128)(2,1)S(1)}, bf16[2,64,1024]{2,1,0:T(8,128)(2,1)S(1)}, u32[]{:S(2)}, u32[]{:S(2)}) collective-permute-start(bf16[2,64,1024]{2,1,0:T(8,128)(2,1)S(1)} %get-tuple-element.85), channel_id=1, source_target_pairs={{0,16},{4,20},{8,24},{12,28},{16,0},{20,4},{24,8},{28,12},{32,48},... | collective-permute-start | bytes 786440 | tf_op jit(solution)/shard_map/ppermute | solution.py:309
  18.4 12.1 %collective-permute-start.7 = (bf16[2,64,1024]{2,1,0:T(8,128)(2,1)S(1)}, bf16[2,64,1024]{2,1,0:T(8,128)(2,1)S(1)}, u32[]{:S(2)}, u32[]{:S(2)}) collective-permute-start(bf16[2,64,1024]{2,1,0:T(8,128)(2,1)S(1)} %get-tuple-element.85), channel_id=1, source_target_pairs={{0,24},{4,28},{8,16},{12,20},{16,8},{20,12},{24,0},{28,4},{32,56},... | collective-permute-start | bytes 786440 | tf_op jit(solution)/shard_map/ppermute | solution.py:309
  18.7 14.5 %collective-permute-start = (bf16[2,128,1024]{2,1,0:T(8,128)(2,1)S(1)}, bf16[2,128,1024]{2,1,0:T(8,128)(2,1)S(1)}, u32[]{:S(2)}, u32[]{:S(2)}) collective-permute-start(bf16[2,128,1024]{2,1,0:T(8,128)(2,1)S(1)} %get-tuple-element.44), channel_id=1, source_target_pairs={{0,4},{4,0},{8,12},{12,8},{16,20},{20,16},{24,28},{28,24},{32,36},... | collective-permute-start | bytes 1572872 | tf_op jit(solution)/shard_map/ppermute | solution.py:309
  18.7 10.6 %collective-permute-start.5 = (bf16[2,32,1024]{2,1,0:T(8,128)(2,1)S(1)}, bf16[2,32,1024]{2,1,0:T(8,128)(2,1)S(1)}, u32[]{:S(2)}, u32[]{:S(2)}) collective-permute-start(bf16[2,32,1024]{2,1,0:T(8,128)(2,1)S(1)} %get-tuple-element.86.rest_1_), channel_id=1, source_target_pairs={{0,8},{4,12},{8,0},{12,4},{16,24},{20,28},{24,16},{28,20},{32,40},... | collective-permute-start | bytes 393224 | tf_op jit(solution)/shard_map/ppermute | solution.py:309
  29.2 1.8 %collective-permute-start.9 = (bf16[2,32,1024]{2,1,0:T(8,128)(2,1)S(1)}, bf16[2,32,1024]{2,1,0:T(8,128)(2,1)S(1)}, u32[]{:S(2)}, u32[]{:S(2)}) collective-permute-start(bf16[2,32,1024]{2,1,0:T(8,128)(2,1)S(1)} %get-tuple-element.86.rest_1_), channel_id=1, source_target_pairs={{0,4},{4,0},{8,12},{12,8},{16,20},{20,16},{24,28},{28,24},{32,36},... | collective-permute-start | bytes 393224 | tf_op jit(solution)/shard_map/ppermute | solution.py:309
  29.6 3.6 %collective-permute-start.8 = (bf16[2,64,1024]{2,1,0:T(8,128)(2,1)S(1)}, bf16[2,64,1024]{2,1,0:T(8,128)(2,1)S(1)}, u32[]{:S(2)}, u32[]{:S(2)}) collective-permute-start(bf16[2,64,1024]{2,1,0:T(8,128)(2,1)S(1)} %collective-permute-done.1.rest_0_), channel_id=1, source_target_pairs={{0,4},{4,0},{8,12},{12,8},{16,20},{20,16},{24,28},{28,24},{32,36},... | collective-permute-start | bytes 786440 | tf_op jit(solution)/shard_map/ppermute | solution.py:309
  30.5 2.6 %collective-permute-start.11 = (bf16[2,64,1024]{2,1,0:T(8,128)(2,1)S(1)}, bf16[2,64,1024]{2,1,0:T(8,128)(2,1)S(1)}, u32[]{:S(2)}, u32[]{:S(2)}) collective-permute-start(bf16[2,64,1024]{2,1,0:T(8,128)(2,1)S(1)} %collective-permute-done.6.rest_3_), channel_id=1, source_target_pairs={{0,4},{4,0},{8,12},{12,8},{16,20},{20,16},{24,28},{28,24},{32,36},... | collective-permute-start | bytes 786440 | tf_op jit(solution)/shard_map/ppermute | solution.py:309
  30.5 2.6 %collective-permute-start.12 = (bf16[2,64,1024]{2,1,0:T(8,128)(2,1)S(1)}, bf16[2,64,1024]{2,1,0:T(8,128)(2,1)S(1)}, u32[]{:S(2)}, u32[]{:S(2)}) collective-permute-start(bf16[2,64,1024]{2,1,0:T(8,128)(2,1)S(1)} %collective-permute-done.7.rest_4_), channel_id=1, source_target_pairs={{0,4},{4,0},{8,12},{12,8},{16,20},{20,16},{24,28},{28,24},{32,36},... | collective-permute-start | bytes 786440 | tf_op jit(solution)/shard_map/ppermute | solution.py:309
  31.0 2.1 %collective-permute-start.10 = (bf16[2,32,1024]{2,1,0:T(8,128)(2,1)S(1)}, bf16[2,32,1024]{2,1,0:T(8,128)(2,1)S(1)}, u32[]{:S(2)}, u32[]{:S(2)}) collective-permute-start(bf16[2,32,1024]{2,1,0:T(8,128)(2,1)S(1)} %collective-permute-done.5.rest_2_), channel_id=1, source_target_pairs={{0,4},{4,0},{8,12},{12,8},{16,20},{20,16},{24,28},{28,24},{32,36},... | collective-permute-start | bytes 393224 | tf_op jit(solution)/shard_map/ppermute | solution.py:309
  33.1 14.1 %copy-start.1 = (f32[1024]{0:T(1024)S(1)}, f32[1024]{0:T(1024)}, u32[]{:S(2)}) copy-start(f32[1024]{0:T(1024)} %param.7) | copy-start | bytes 12292
  38.1 6.5 %collective-permute-start.13 = (f32[8,256]{1,0:T(8,128)S(1)}, f32[8,256]{1,0:T(8,128)S(1)}, u32[]{:S(2)}, u32[]{:S(2)}) collective-permute-start(f32[8,256]{1,0:T(8,128)S(1)} %get-tuple-element.82.s0), channel_id=1, source_target_pairs={{0,1},{1,2},{2,3},{3,0},{4,5},{5,6},{6,7},{7,4},{8,9},{9,10},{10,1... | collective-permute-start | bytes 24584 | tf_op jit(solution)/shard_map/ppermute | solution.py:334
  40.0 5.3 %collective-permute-start.14 = (f32[8,256]{1,0:T(8,128)S(1)}, f32[8,256]{1,0:T(8,128)S(1)}, u32[]{:S(2)}, u32[]{:S(2)}) collective-permute-start(f32[8,256]{1,0:T(8,128)S(1)} %get-tuple-element.82.s0), channel_id=1, source_target_pairs={{0,2},{1,3},{2,0},{3,1},{4,6},{5,7},{6,4},{7,5},{8,10},{9,11},{10,... | collective-permute-start | bytes 24584 | tf_op jit(solution)/shard_map/ppermute | solution.py:334
  43.6 3.7 %collective-permute-start.15 = (f32[8,256]{1,0:T(8,128)S(1)}, f32[8,256]{1,0:T(8,128)S(1)}, u32[]{:S(2)}, u32[]{:S(2)}) collective-permute-start(f32[8,256]{1,0:T(8,128)S(1)} %get-tuple-element.82.s0), channel_id=1, source_target_pairs={{0,3},{1,0},{2,1},{3,2},{4,7},{5,4},{6,5},{7,6},{8,11},{9,8},{10,9... | collective-permute-start | bytes 24584 | tf_op jit(solution)/shard_map/ppermute | solution.py:334

commit v4 on v3

--- a/solution.py
+++ b/solution.py
@@ -37,7 +37,7 @@
     shape = (rows, rows)
     per = rows // slabs
     row = iota2(shape, 0)
-    source = (row % per) * slabs + row // per
+    source = (row & (per - 1)) * slabs + (row >> (per.bit_length() - 1))
     return jnp.where(iota2(shape, 1) == source, 1.0, 0.0).astype(BF16)
 
 
@@ -276,17 +276,20 @@
 
 def norm_kernel(features, att_ref, s0, s1, s2, s3, gain_ref, out_hbm, out_vmem, sems):
     shape = (GROUP, GROUP)
-    source = (iota2(shape, 0) % 16) * 16 + iota2(shape, 0) // 16
+    source = (iota2(shape, 0) & 15) * 16 + (iota2(shape, 0) >> 4)
     hit = iota2(shape, 1) == source
     scale = lax.rsqrt(((s0[...] + s1[...]) + (s2[...] + s3[...])) / features + 1e-06)
     copies = []
-    for group in range(att_ref.shape[0] // GROUP):
-        rows = pl.ds(group * GROUP, GROUP)
-        matrix = jnp.where(hit, scale[group : group + 1], 0.0).astype(BF16)
-        mixed = jnp.dot(matrix, att_ref[rows, :], preferred_element_type=F32)
-        out_vmem[rows, :] = (mixed * gain_ref[...]).astype(BF16)
-        copies.append(pltpu.make_async_copy(out_vmem.at[rows], out_hbm.at[rows], sems.at[group]))
-        copies[-1].start()
+    for first in range(0, att_ref.shape[0] // GROUP, TOGETHER):
+        for group in range(first, first + TOGETHER):
+            rows = pl.ds(group * GROUP, GROUP)
+            matrix = jnp.where(hit, scale[group : group + 1], 0.0).astype(BF16)
+            mixed = jnp.dot(matrix, att_ref[rows, :], preferred_element_type=F32)
+            out_vmem[rows, :] = (mixed * gain_ref[...]).astype(BF16)
+        for group in range(first, first + TOGETHER):
+            rows = pl.ds(group * GROUP, GROUP)
+            copies.append(pltpu.make_async_copy(out_vmem.at[rows], out_hbm.at[rows], sems.at[group]))
+            copies[-1].start()
     for copy in copies:
         copy.wait()
 

time: 50.6 us -> 50.8 us (level)
  no operation moved by 1% of the time
where the time goes in v4:
time: 50.8 us; the launch traced here: 49.9 us
  Pallas kernels  28.6 us (56%)
  starting transfers between devices  17.6 us (35%)
  waiting for transfers between devices  3.35 us (7%)
    pallas_call x3, Pallas kernels, near(): pl.pallas_call(functools.partial(near_kernel, start), in_specs=[pl.BlockS...  16.4 us
    ppermute x13, starting transfers between devices, swapped(): lax.ppermute(array, axis, [(i, i ^ bits) for i in range(lax.axis_size(axi...  11 us
    ppermute x3, starting transfers between devices, local(): lax.ppermute(squares, 'head', [(i, (i + s) % 4) for i in range(4)])  6.52 us
    pallas_call x1, Pallas kernels, far(): pl.pallas_call(far_kernel, in_specs=[whole] * len(operands), out_specs=[w...  4.89 us
    pallas_call x1, Pallas kernels, pool(): pl.pallas_call(pool_kernel, in_specs=[pl.BlockSpec(memory_space=pl.ANY)]...  4.83 us
    ppermute x3, waiting for transfers between devices, local(): lax.ppermute(squares, 'head', [(i, (i + s) % 4) for i in range(4)])  2.64 us
    pallas_call x1, Pallas kernels, normed(): pl.pallas_call(functools.partial(norm_kernel, features), in_specs=[whole]...  2.51 us
  transfers between devices with their start and end apart: 16, of which 3 were waited for; matrix products, arithmetic and copies ran while one was open for 0% of the time, Pallas kernels for 33%

profile of v4, /device:TPU:2, one launch (start us, length us, event | category | flops | bytes accessed | tf_op | source)
XLA Modules:
  0.0 49.9 jit_solution(7022121199356155262)
XLA Ops:
  0.0 0.0 copy-start
  0.0 4.8 %pool.1 = (bf16[2048,1024]{1,0:T(8,128)(2,1)S(1)}, bf16[2048,1024]{1,0:T(8,128)(2,1)S(1)}, bf16[1024,1024]{1,0:T(8,128)(2,1)S(1)}, bf16[1024,1024]{1,0:T(8,128)(...) custom-call(bf16[2048,1024]{1,0:T(8,128)(2,1)} %k_hbm.1, ...), custom_call_target="tpu_custom_call" | custom-call | flops 2147483648 | bytes 8388608 | tf_op jit(solution)/shard_map/pool/pallas_call | solution.py:130
  4.8 2.2 %collective-permute-start.3 = (bf16[2,8,1024]{2,1,0:T(8,128)(2,1)S(1)}, bf16[2,8,1024]{2,1,0:T(8,128)(2,1)S(1)}, u32[]{:S(2)}, u32[]{:S(2)}) collective-permute-start(bf16[2,8,1024]{2,1,0:T(8,128)(2,1)S(1)} %slice.3), channel_id=1, source_target_pairs={{0,64},{4,68},{8,72},{12,76},{16,80},{20,84},{24,88},{28,92},{32,9... | collective-permute-start | bytes 98312 | tf_op jit(solution)/shard_map/ppermute | solution.py:312
  7.1 0.0 collective-permute-start.4
  7.1 2.6 %collective-permute-start.2 = (bf16[2,16,1024]{2,1,0:T(8,128)(2,1)S(1)}, bf16[2,16,1024]{2,1,0:T(8,128)(2,1)S(1)}, u32[]{:S(2)}, u32[]{:S(2)}) collective-permute-start(bf16[2,16,1024]{2,1,0:T(8,128)(2,1)S(1)} %get-tuple-element.48), channel_id=1, source_target_pairs={{0,32},{4,36},{8,40},{12,44},{16,48},{20,52},{24,56},{28,60},{32,0... | collective-permute-start | bytes 196616 | tf_op jit(solution)/shard_map/ppermute | solution.py:312
  9.6 1.6 %collective-permute-start.1 = (bf16[2,64,1024]{2,1,0:T(8,128)(2,1)S(1)}, bf16[2,64,1024]{2,1,0:T(8,128)(2,1)S(1)}, u32[]{:S(2)}, u32[]{:S(2)}) collective-permute-start(bf16[2,64,1024]{2,1,0:T(8,128)(2,1)S(1)} %get-tuple-element.45), channel_id=1, source_target_pairs={{0,8},{4,12},{8,0},{12,4},{16,24},{20,28},{24,16},{28,20},{32,40},... | collective-permute-start | bytes 786440 | tf_op jit(solution)/shard_map/ppermute | solution.py:312
  11.2 0.0 copy-done
  11.2 4.1 %near.3 = (bf16[512,1024]{1,0:T(8,128)(2,1)S(1)}, f32[512,128]{1,0:T(8,128)S(1)}, bf16[32,1024]{1,0:T(8,128)(2,1)S(1)}) custom-call(bf16[2048,1024]{1,0:T(8,128)(2,1)S(1)} %copy-done, bf16[2048,1024]{1,0:T(8,128)(2,1)S(1)} %get-tuple-element.51.k0, bf16[2048,1024]{1,0:T(8,128)(2,1)S(1)} %get-tuple-element.52.v0, ...), custom_call_target="tpu_custom_call" | custom-call | flops 1073741824 | bytes 6291456 | tf_op jit(solution)/shard_map/near/pallas_call | solution.py:177
  15.4 0.0 collective-permute-done.3
  15.4 0.0 collective-permute-done.4
  15.4 0.0 collective-permute-done.2
  15.5 3.0 %collective-permute-start.6 = (bf16[2,64,1024]{2,1,0:T(8,128)(2,1)S(1)}, bf16[2,64,1024]{2,1,0:T(8,128)(2,1)S(1)}, u32[]{:S(2)}, u32[]{:S(2)}) collective-permute-start(bf16[2,64,1024]{2,1,0:T(8,128)(2,1)S(1)} %get-tuple-element.85), channel_id=1, source_target_pairs={{0,16},{4,20},{8,24},{12,28},{16,0},{20,4},{24,8},{28,12},{32,48},... | collective-permute-start | bytes 786440 | tf_op jit(solution)/shard_map/ppermute | solution.py:312
  18.4 0.2 collective-permute-start.7
  18.7 0.0 collective-permute-start
  18.7 0.4 collective-permute-start.5
  19.0 10.2 %near.4 = (bf16[1280,1024]{1,0:T(8,128)(2,1)S(1)}, f32[1280,128]{1,0:T(8,128)S(1)}, bf16[80,1024]{1,0:T(8,128)(2,1)S(1)}) custom-call(bf16[2048,1024]{1,0:T(8,128)(2,1)S(1)} %copy-done, bf16[2048,1024]{1,0:T(8,128)(2,1)S(1)} %get-tuple-element.51.k0, bf16[2048,1024]{1,0:T(8,128)(2,1)S(1)} %get-tuple-element.52.v0, ...), custom_call_target="tpu_custom_call" | custom-call | flops 2684354560 | bytes 15728640 | tf_op jit(solution)/shard_map/near/pallas_call | solution.py:177
  29.2 0.0 collective-permute-done.5.rest_2_
  29.2 0.3 collective-permute-start.9
  29.5 0.0 collective-permute-done.1.rest_0_
  29.6 0.3 collective-permute-start.8
  29.8 0.0 collective-permute-done.6.rest_3_
  29.8 0.7 %collective-permute-done.7.rest_4_ = bf16[2,64,1024]{2,1,0:T(8,128)(2,1)S(1)} collective-permute-done((bf16[2,64,1024]{2,1,0:T(8,128)(2,1)S(1)}, bf16[2,64,1024]{2,1,0:T(8,128)(2,1)S(1)}, u32[]{:S(2)}, u32[]{:S(2)}) %collective-permute-start.7) | collective-permute-done | bytes 262176 | tf_op jit(solution)/shard_map/ppermute | solution.py:312
  30.5 0.0 collective-permute-start.11
  30.5 0.5 collective-permute-start.12
  31.0 0.0 collective-permute-done.9.rest_6_
  31.0 0.0 collective-permute-start.10
  31.1 2.0 %near.5 = (bf16[256,1024]{1,0:T(8,128)(2,1)S(1)}, f32[256,128]{1,0:T(8,128)S(1)}, bf16[16,1024]{1,0:T(8,128)(2,1)S(1)}) custom-call(bf16[2048,1024]{1,0:T(8,128)(2,1)S(1)} %copy-done, bf16[2048,1024]{1,0:T(8,128)(2,1)S(1)} %get-tuple-element.51.k0, bf16[2048,1024]{1,0:T(8,128)(2,1)S(1)} %get-tuple-element.52.v0, ...), custom_call_target="tpu_custom_call" | custom-call | flops 536870912 | bytes 3145728 | tf_op jit(solution)/shard_map/near/pallas_call | solution.py:177
  33.1 0.0 copy-start.1
  33.1 0.0 collective-permute-done.10.rest_7_
  33.1 0.0 collective-permute-done.8.rest_5_
  33.1 0.0 collective-permute-done.s4
  33.1 0.0 collective-permute-done.11.rest_8_
  33.2 0.0 collective-permute-done.12.rest_9_
  33.2 4.9 %far.1 = (bf16[2048,1024]{1,0:T(8,128)(2,1)S(1)}, f32[8,256]{1,0:T(8,128)S(1)}) custom-call(bf16[2,128,1024]{2,1,0:T(8,128)(2,1)S(1)} %collective-permute-done.s4, bf16[2,64,1024]{2,1,0:T(8,128)(2,1)S(1)} %collective-permute-done.1.rest_0_, bf16[2,32,1024]{2,1,0:T(8,128)(2,1)S(1)} %get-tuple-element.86.rest_1_, ...), custom_call_target="tpu_custom_call" | custom-call | tf_op jit(solution)/shard_map/far/pallas_call | solution.py:266
  38.1 1.9 %collective-permute-start.13 = (f32[8,256]{1,0:T(8,128)S(1)}, f32[8,256]{1,0:T(8,128)S(1)}, u32[]{:S(2)}, u32[]{:S(2)}) collective-permute-start(f32[8,256]{1,0:T(8,128)S(1)} %get-tuple-element.82.s0), channel_id=1, source_target_pairs={{0,1},{1,2},{2,3},{3,0},{4,5},{5,6},{6,7},{7,4},{8,9},{9,10},{10,1... | collective-permute-start | bytes 24584 | tf_op jit(solution)/shard_map/ppermute | solution.py:337
  40.0 3.6 %collective-permute-start.14 = (f32[8,256]{1,0:T(8,128)S(1)}, f32[8,256]{1,0:T(8,128)S(1)}, u32[]{:S(2)}, u32[]{:S(2)}) collective-permute-start(f32[8,256]{1,0:T(8,128)S(1)} %get-tuple-element.82.s0), channel_id=1, source_target_pairs={{0,2},{1,3},{2,0},{3,1},{4,6},{5,7},{6,4},{7,5},{8,10},{9,11},{10,... | collective-permute-start | bytes 24584 | tf_op jit(solution)/shard_map/ppermute | solution.py:337
  43.6 1.0 %collective-permute-start.15 = (f32[8,256]{1,0:T(8,128)S(1)}, f32[8,256]{1,0:T(8,128)S(1)}, u32[]{:S(2)}, u32[]{:S(2)}) collective-permute-start(f32[8,256]{1,0:T(8,128)S(1)} %get-tuple-element.82.s0), channel_id=1, source_target_pairs={{0,3},{1,0},{2,1},{3,2},{4,7},{5,4},{6,5},{7,6},{8,11},{9,8},{10,9... | collective-permute-start | bytes 24584 | tf_op jit(solution)/shard_map/ppermute | solution.py:337
  44.6 0.0 collective-permute-done.13.s1
  44.6 0.7 %collective-permute-done.14.s2 = f32[8,256]{1,0:T(8,128)S(1)} collective-permute-done((f32[8,256]{1,0:T(8,128)S(1)}, f32[8,256]{1,0:T(8,128)S(1)}, u32[]{:S(2)}, u32[]{:S(2)}) %collective-permute-start.14) | collective-permute-done | bytes 8224 | tf_op jit(solution)/shard_map/ppermute | solution.py:337
  45.3 1.9 %collective-permute-done.15.s3 = f32[8,256]{1,0:T(8,128)S(1)} collective-permute-done((f32[8,256]{1,0:T(8,128)S(1)}, f32[8,256]{1,0:T(8,128)S(1)}, u32[]{:S(2)}, u32[]{:S(2)}) %collective-permute-start.15) | collective-permute-done | bytes 8224 | tf_op jit(solution)/shard_map/ppermute | solution.py:337
  47.2 0.0 copy-done.1
  47.2 2.5 %norm.1 = bf16[2048,1024]{1,0:T(8,128)(2,1)} custom-call(bf16[2048,1024]{1,0:T(8,128)(2,1)S(1)} %get-tuple-element.81.att_ref, f32[8,256]{1,0:T(8,128)S(1)} %get-tuple-element.82.s0, f32[8,256]{1,0:T(8,128)S(1)} %collective-permute-done.13.s1, f32[8,256]{1,0:T(8,128)S(1)} %collective-permute-done.14.s2, f32[8,256]{1,0:T(8,128)S(1)} %collective-permute-done.15.s3, ...), custom_call_target="tpu_custom_call" | custom-call | tf_op jit(solution)/shard_map/norm/pallas_call | solution.py:300
  (5 shorter events, 0.0 us)
Async XLA Ops:
  0.0 11.2 %copy-start = (bf16[2048,1024]{1,0:T(8,128)(2,1)S(1)}, bf16[2048,1024]{1,0:T(8,128)(2,1)}, u32[]{:S(2)}) copy-start(bf16[2048,1024]{1,0:T(8,128)(2,1)} %q_ref.2) | copy-start | bytes 12582916
  4.8 10.5 %collective-permute-start.3 = (bf16[2,8,1024]{2,1,0:T(8,128)(2,1)S(1)}, bf16[2,8,1024]{2,1,0:T(8,128)(2,1)S(1)}, u32[]{:S(2)}, u32[]{:S(2)}) collective-permute-start(bf16[2,8,1024]{2,1,0:T(8,128)(2,1)S(1)} %slice.3), channel_id=1, source_target_pairs={{0,64},{4,68},{8,72},{12,76},{16,80},{20,84},{24,88},{28,92},{32,9... | collective-permute-start | bytes 98312 | tf_op jit(solution)/shard_map/ppermute | solution.py:312
  7.1 8.3 %collective-permute-start.4 = (bf16[2,8,1024]{2,1,0:T(8,128)(2,1)S(1)}, bf16[2,8,1024]{2,1,0:T(8,128)(2,1)S(1)}, u32[]{:S(2)}, u32[]{:S(2)}) collective-permute-start(bf16[2,8,1024]{2,1,0:T(8,128)(2,1)S(1)} %slice.3), channel_id=1, source_target_pairs={{0,96},{4,100},{8,104},{12,108},{16,112},{20,116},{24,120},{28,124... | collective-permute-start | bytes 98312 | tf_op jit(solution)/shard_map/ppermute | solution.py:312
  7.1 8.3 %collective-permute-start.2 = (bf16[2,16,1024]{2,1,0:T(8,128)(2,1)S(1)}, bf16[2,16,1024]{2,1,0:T(8,128)(2,1)S(1)}, u32[]{:S(2)}, u32[]{:S(2)}) collective-permute-start(bf16[2,16,1024]{2,1,0:T(8,128)(2,1)S(1)} %get-tuple-element.48), channel_id=1, source_target_pairs={{0,32},{4,36},{8,40},{12,44},{16,48},{20,52},{24,56},{28,60},{32,0... | collective-permute-start | bytes 196616 | tf_op jit(solution)/shard_map/ppermute | solution.py:312
  9.6 19.9 %collective-permute-start.1 = (bf16[2,64,1024]{2,1,0:T(8,128)(2,1)S(1)}, bf16[2,64,1024]{2,1,0:T(8,128)(2,1)S(1)}, u32[]{:S(2)}, u32[]{:S(2)}) collective-permute-start(bf16[2,64,1024]{2,1,0:T(8,128)(2,1)S(1)} %get-tuple-element.45), channel_id=1, source_target_pairs={{0,8},{4,12},{8,0},{12,4},{16,24},{20,28},{24,16},{28,20},{32,40},... | collective-permute-start | bytes 786440 | tf_op jit(solution)/shard_map/ppermute | solution.py:312
  15.5 14.4 %collective-permute-start.6 = (bf16[2,64,1024]{2,1,0:T(8,128)(2,1)S(1)}, bf16[2,64,1024]{2,1,0:T(8,128)(2,1)S(1)}, u32[]{:S(2)}, u32[]{:S(2)}) collective-permute-start(bf16[2,64,1024]{2,1,0:T(8,128)(2,1)S(1)} %get-tuple-element.85), channel_id=1, source_target_pairs={{0,16},{4,20},{8,24},{12,28},{16,0},{20,4},{24,8},{28,12},{32,48},... | collective-permute-start | bytes 786440 | tf_op jit(solution)/shard_map/ppermute | solution.py:312
  18.4 12.1 %collective-permute-start.7 = (bf16[2,64,1024]{2,1,0:T(8,128)(2,1)S(1)}, bf16[2,64,1024]{2,1,0:T(8,128)(2,1)S(1)}, u32[]{:S(2)}, u32[]{:S(2)}) collective-permute-start(bf16[2,64,1024]{2,1,0:T(8,128)(2,1)S(1)} %get-tuple-element.85), channel_id=1, source_target_pairs={{0,24},{4,28},{8,16},{12,20},{16,8},{20,12},{24,0},{28,4},{32,56},... | collective-permute-start | bytes 786440 | tf_op jit(solution)/shard_map/ppermute | solution.py:312
  18.7 14.5 %collective-permute-start = (bf16[2,128,1024]{2,1,0:T(8,128)(2,1)S(1)}, bf16[2,128,1024]{2,1,0:T(8,128)(2,1)S(1)}, u32[]{:S(2)}, u32[]{:S(2)}) collective-permute-start(bf16[2,128,1024]{2,1,0:T(8,128)(2,1)S(1)} %get-tuple-element.44), channel_id=1, source_target_pairs={{0,4},{4,0},{8,12},{12,8},{16,20},{20,16},{24,28},{28,24},{32,36},... | collective-permute-start | bytes 1572872 | tf_op jit(solution)/shard_map/ppermute | solution.py:312
  18.7 10.6 %collective-permute-start.5 = (bf16[2,32,1024]{2,1,0:T(8,128)(2,1)S(1)}, bf16[2,32,1024]{2,1,0:T(8,128)(2,1)S(1)}, u32[]{:S(2)}, u32[]{:S(2)}) collective-permute-start(bf16[2,32,1024]{2,1,0:T(8,128)(2,1)S(1)} %get-tuple-element.86.rest_1_), channel_id=1, source_target_pairs={{0,8},{4,12},{8,0},{12,4},{16,24},{20,28},{24,16},{28,20},{32,40},... | collective-permute-start | bytes 393224 | tf_op jit(solution)/shard_map/ppermute | solution.py:312
  29.2 1.8 %collective-permute-start.9 = (bf16[2,32,1024]{2,1,0:T(8,128)(2,1)S(1)}, bf16[2,32,1024]{2,1,0:T(8,128)(2,1)S(1)}, u32[]{:S(2)}, u32[]{:S(2)}) collective-permute-start(bf16[2,32,1024]{2,1,0:T(8,128)(2,1)S(1)} %get-tuple-element.86.rest_1_), channel_id=1, source_target_pairs={{0,4},{4,0},{8,12},{12,8},{16,20},{20,16},{24,28},{28,24},{32,36},... | collective-permute-start | bytes 393224 | tf_op jit(solution)/shard_map/ppermute | solution.py:312
  29.6 3.6 %collective-permute-start.8 = (bf16[2,64,1024]{2,1,0:T(8,128)(2,1)S(1)}, bf16[2,64,1024]{2,1,0:T(8,128)(2,1)S(1)}, u32[]{:S(2)}, u32[]{:S(2)}) collective-permute-start(bf16[2,64,1024]{2,1,0:T(8,128)(2,1)S(1)} %collective-permute-done.1.rest_0_), channel_id=1, source_target_pairs={{0,4},{4,0},{8,12},{12,8},{16,20},{20,16},{24,28},{28,24},{32,36},... | collective-permute-start | bytes 786440 | tf_op jit(solution)/shard_map/ppermute | solution.py:312
  30.5 2.6 %collective-permute-start.11 = (bf16[2,64,1024]{2,1,0:T(8,128)(2,1)S(1)}, bf16[2,64,1024]{2,1,0:T(8,128)(2,1)S(1)}, u32[]{:S(2)}, u32[]{:S(2)}) collective-permute-start(bf16[2,64,1024]{2,1,0:T(8,128)(2,1)S(1)} %collective-permute-done.6.rest_3_), channel_id=1, source_target_pairs={{0,4},{4,0},{8,12},{12,8},{16,20},{20,16},{24,28},{28,24},{32,36},... | collective-permute-start | bytes 786440 | tf_op jit(solution)/shard_map/ppermute | solution.py:312
  30.5 2.6 %collective-permute-start.12 = (bf16[2,64,1024]{2,1,0:T(8,128)(2,1)S(1)}, bf16[2,64,1024]{2,1,0:T(8,128)(2,1)S(1)}, u32[]{:S(2)}, u32[]{:S(2)}) collective-permute-start(bf16[2,64,1024]{2,1,0:T(8,128)(2,1)S(1)} %collective-permute-done.7.rest_4_), channel_id=1, source_target_pairs={{0,4},{4,0},{8,12},{12,8},{16,20},{20,16},{24,28},{28,24},{32,36},... | collective-permute-start | bytes 786440 | tf_op jit(solution)/shard_map/ppermute | solution.py:312
  31.0 2.1 %collective-permute-start.10 = (bf16[2,32,1024]{2,1,0:T(8,128)(2,1)S(1)}, bf16[2,32,1024]{2,1,0:T(8,128)(2,1)S(1)}, u32[]{:S(2)}, u32[]{:S(2)}) collective-permute-start(bf16[2,32,1024]{2,1,0:T(8,128)(2,1)S(1)} %collective-permute-done.5.rest_2_), channel_id=1, source_target_pairs={{0,4},{4,0},{8,12},{12,8},{16,20},{20,16},{24,28},{28,24},{32,36},... | collective-permute-start | bytes 393224 | tf_op jit(solution)/shard_map/ppermute | solution.py:312
  33.1 14.1 %copy-start.1 = (f32[1024]{0:T(1024)S(1)}, f32[1024]{0:T(1024)}, u32[]{:S(2)}) copy-start(f32[1024]{0:T(1024)} %param.7) | copy-start | bytes 12292
  38.1 6.5 %collective-permute-start.13 = (f32[8,256]{1,0:T(8,128)S(1)}, f32[8,256]{1,0:T(8,128)S(1)}, u32[]{:S(2)}, u32[]{:S(2)}) collective-permute-start(f32[8,256]{1,0:T(8,128)S(1)} %get-tuple-element.82.s0), channel_id=1, source_target_pairs={{0,1},{1,2},{2,3},{3,0},{4,5},{5,6},{6,7},{7,4},{8,9},{9,10},{10,1... | collective-permute-start | bytes 24584 | tf_op jit(solution)/shard_map/ppermute | solution.py:337
  40.0 5.3 %collective-permute-start.14 = (f32[8,256]{1,0:T(8,128)S(1)}, f32[8,256]{1,0:T(8,128)S(1)}, u32[]{:S(2)}, u32[]{:S(2)}) collective-permute-start(f32[8,256]{1,0:T(8,128)S(1)} %get-tuple-element.82.s0), channel_id=1, source_target_pairs={{0,2},{1,3},{2,0},{3,1},{4,6},{5,7},{6,4},{7,5},{8,10},{9,11},{10,... | collective-permute-start | bytes 24584 | tf_op jit(solution)/shard_map/ppermute | solution.py:337
  43.6 3.7 %collective-permute-start.15 = (f32[8,256]{1,0:T(8,128)S(1)}, f32[8,256]{1,0:T(8,128)S(1)}, u32[]{:S(2)}, u32[]{:S(2)}) collective-permute-start(f32[8,256]{1,0:T(8,128)S(1)} %get-tuple-element.82.s0), channel_id=1, source_target_pairs={{0,3},{1,0},{2,1},{3,2},{4,7},{5,4},{6,5},{7,6},{8,11},{9,8},{10,9... | collective-permute-start | bytes 24584 | tf_op jit(solution)/shard_map/ppermute | solution.py:337
